TPU v7x, 256 devices: a whole 4x4x8 slice. The times are simulated.
256 devices in a mesh: ao: 16 (over x_hi, z), pair: 16 (over y, x_lo, core).
Axes of the slice: x: 4 (x_hi: 2, x_lo: 2; x = x_hi * 2 + x_lo), y: 4, z: 8, core: 2. Of those that a mesh axis runs over, the one named last changes fastest.
Arguments:
- green_occ: bfloat16 [2048, 2048], P(None, 'ao'), may hold values from -0.75 to 0.75
- green_virtual: bfloat16 [2048, 2048], P(None, 'ao'), may hold values from -0.75 to 0.75
- tile_values: bfloat16 [4096, 64, 128], P(('ao', 'pair')), may hold values from -0.4375 to 0.4375
- tile_orbital: int32 [4096], P(('ao', 'pair')), may hold values from 0 to 31
- tile_window: int32 [4096], P(('ao', 'pair')), may hold values from 0 to 15
- tile_count: int32 [256], P(('ao', 'pair')), may hold values from 1 to 16, as said below
Outputs:
- polarizability: float32 [8192, 1536], P(('ao', 'pair'))
Inputs may be any that keep to these rules, and one draw needn't show every extreme that they name: `tile_count`: some row group in every draw has all 16 slots live.
All inputs are finite; a program needn't handle non-finite values.
Results may differ from a plain program's by a relative error of at most 0.0041.
Values may be sent and summed in bfloat16 or wider, within the bound.
No kernel may reach another device: no remote copies, remote signals or barrier semaphores. Data moves between devices by JAX's collectives and lax.ppermute only.
A program may use at most 64 MiB of HBM per device.

v0:
```python
import jax
import jax.numpy as jnp
from jax import lax
from jax.sharding import PartitionSpec as P

RHB = 8


def shifted(value, axis, steps):
    count = lax.axis_size(axis)
    pairs = [(source, (source + steps) % count) for source in range(count)]
    return lax.ppermute(value, axis, pairs)


def moment_rows(green_part, tile_values, tile_orbital, onehot):
    orbitals = green_part.shape[0]
    column_span = green_part.shape[1]
    block_size = tile_values.shape[1]
    lam_rows = tile_values.shape[2] // block_size
    windows = onehot.shape[1]
    picked_rows = green_part.reshape(orbitals // block_size, block_size, column_span)[tile_orbital]
    product = jnp.einsum(
        "cjs,cjx->csx", picked_rows, tile_values, preferred_element_type=jnp.float32
    )
    product = product.reshape(product.shape[0], column_span, lam_rows, block_size)
    moment = jnp.einsum("csiq,cr->sirq", product, onehot, precision=lax.Precision.HIGHEST)
    return moment.reshape(column_span * lam_rows, windows * block_size).astype(jnp.bfloat16)


def per_device(green_occ, green_virtual, tile_values, tile_orbital, tile_window, tile_count):
    block_size = tile_values.shape[1]
    own_width = green_occ.shape[1]
    windows = 2 * RHB
    window_width = windows * block_size
    home_rows = RHB * block_size
    live_count = tile_count[0]
    live_slots = jnp.arange(tile_values.shape[0], dtype=jnp.int32) < live_count
    targets = jnp.arange(windows, dtype=jnp.int32)
    onehot = ((tile_window[:, None] == targets[None, :]) & live_slots[:, None]).astype(jnp.float32)

    def pair_up(running_sum, occ_part, vir_part):
        occ_moment = moment_rows(occ_part, tile_values, tile_orbital, onehot)
        vir_moment = moment_rows(vir_part, tile_values, tile_orbital, onehot)
        product = lax.dot_general(
            occ_moment, vir_moment, (((0,), (0,)), ((), ())), preferred_element_type=jnp.float32
        )
        return running_sum + product

    initial = jnp.zeros((window_width, window_width), jnp.float32)
    occ_piece = lax.all_gather(green_occ, "ao", axis=1, tiled=True)
    vir_piece = lax.all_gather(green_virtual, "ao", axis=1, tiled=True)
    column_span = occ_piece.shape[1]

    def step_shard(index_shard, running):
        offset = index_shard * own_width
        occ_slice = lax.dynamic_slice_in_dim(occ_piece, offset, own_width, 1)
        vir_slice = lax.dynamic_slice_in_dim(vir_piece, offset, own_width, 1)
        return pair_up(running, occ_slice, vir_slice)

    partial_chi = lax.fori_loop(0, column_span // own_width, step_shard, initial)
    halves = partial_chi.reshape(2, home_rows, window_width)
    summed = lax.psum_scatter(halves, "pair", scatter_dimension=1, tiled=True)
    upper_band = summed[0]
    lower_band = shifted(summed[1], "ao", 1)
    return jnp.concatenate(
        [
            lower_band[:, :home_rows],
            lower_band[:, home_rows:] + upper_band[:, :home_rows],
            upper_band[:, home_rows:],
        ],
        axis=1,
    )


def solution(mesh):
    in_specs = (
        P(None, "ao"),
        P(None, "ao"),
        P(("ao", "pair"), None, None),
        P(("ao", "pair")),
        P(("ao", "pair")),
        P(("ao", "pair")),
    )
    out_specs = P(("ao", "pair"), None)
    return jax.shard_map(
        per_device, mesh=mesh, in_specs=in_specs, out_specs=out_specs, check_vma=False
    )
```

profile of v0, /device:TPU:6, one launch (start us, length us, event | category | flops | bytes accessed | tf_op | source)
XLA Modules:
  0.0 669.7 jit_solution(13959347363540675124)
XLA Ops:
  8.7 150.3 %all-gather.3.cloned.1.call-done = bf16[2048,2048]{1,0:T(8,128)(2,1)} async-done(((bf16[2048,128]{1,0:T(8,128)(2,1)}), bf16[2048,2048]{1,0:T(8,128)(2,1)}) %all-gather.3.cloned.1.call-update) | async-done | bytes 8388624 | tf_op jit(solution)/shard_map/all_gather | solution.py:50
  159.1 146.8 %all-gather.5.cloned.1.call-done = bf16[2048,2048]{1,0:T(8,128)(2,1)} async-done(((bf16[2048,128]{1,0:T(8,128)(2,1)}), bf16[2048,2048]{1,0:T(8,128)(2,1)}) %all-gather.5.cloned.1.call-update) | async-done | bytes 8388624 | tf_op jit(solution)/shard_map/all_gather | solution.py:51
  305.9 280.8 %while.14 = (s32[]{:T(128)}, f32[1024,1024]{1,0:T(8,128)}, bf16[2048,2048]{1,0:T(8,128)(2,1)}, s32[16]{0:T(128)}, bf16[16,64,128]{2,1,0:T(8,128)(2,1)}, /*index=...) while((s32[]{:T(128)}, f32[1024,1024]{1,0:T(8,128)}, ...), condition=%wide.region_1.0_spmd.clone, body=%wide.region_0.0_spmd.clone.sunk | while | flops 707267136 | bytes 24122320 | solution.py:60
  310.4 1.6 fusion.56
  312.0 1.6 copy.25
  316.3 1.6 copy.24
  318.7 2.7 select_add_fusion.2
  327.5 1.6 copy.25
  330.2 1.6 fusion.54
  331.8 1.6 copy.24
  334.2 4.9 select_add_fusion.2
  345.2 1.6 copy.25
  347.9 1.6 fusion.54
  349.5 1.6 copy.24
  351.9 4.9 select_add_fusion.2
  362.9 1.6 copy.25
  367.2 1.6 copy.24
  369.6 4.9 select_add_fusion.2
  379.0 1.6 fusion.56
  380.6 1.6 copy.25
  383.3 1.6 fusion.54
  384.9 1.6 copy.24
  387.3 4.9 select_add_fusion.2
  398.3 1.6 copy.25
  402.6 1.6 copy.24
  405.0 4.9 select_add_fusion.2
  414.4 1.6 fusion.56
  416.0 1.6 copy.25
  420.3 1.6 copy.24
  422.6 4.9 select_add_fusion.2
  433.6 1.6 copy.25
  438.0 1.6 copy.24
  440.3 4.9 select_add_fusion.2
  449.7 1.6 fusion.56
  451.3 1.6 copy.25
  455.7 1.6 copy.24
  458.0 4.9 select_add_fusion.2
  467.4 1.6 fusion.56
  469.0 1.6 copy.25
  473.4 1.6 copy.24
  475.7 4.9 select_add_fusion.2
  485.1 1.6 fusion.56
  486.7 1.6 copy.25
  491.0 1.6 copy.24
  493.4 4.9 select_add_fusion.2
  502.8 1.6 fusion.56
  504.4 1.6 copy.25
  508.7 1.6 copy.24
  511.1 4.9 select_add_fusion.2
  522.1 1.6 copy.25
  526.4 1.6 copy.24
  528.8 4.9 select_add_fusion.2
  538.2 1.6 fusion.56
  539.8 1.6 copy.25
  544.1 1.6 copy.24
  546.5 4.9 select_add_fusion.2
  557.5 1.6 copy.25
  561.8 1.6 copy.24
  564.2 4.9 select_add_fusion.2
  575.2 1.6 copy.25
  579.5 1.6 copy.24
  581.8 4.9 select_add_fusion.2
  586.8 66.0 %reduce-scatter.2.cloned.1.call-done = f32[2,32,1024]{2,1,0:T(8,128)} async-done(((f32[2,512,1024]{2,1,0:T(8,128)}), f32[2,32,1024]{2,1,0:T(8,128)}) %reduce-scatter.2.cloned.1.call-update) | async-done | bytes 262160 | tf_op jit(solution)/shard_map/reduce_scatter | solution.py:62
  655.3 7.1 %collective-permute-done = f32[32,1024]{1,0:T(8,128)S(1)} collective-permute-done((f32[32,1024]{1,0:T(8,128)S(1)}, f32[32,1024]{1,0:T(8,128)S(1)}, u32[]{:S(2)}, u32[]{:S(2)}) %collective-permute-start) | collective-permute-done | bytes 131104 | tf_op jit(solution)/shard_map/ppermute | solution.py:12
  (241 shorter events, 138.3 us)
Async XLA Ops:
  6.5 152.5 %all-gather.3.cloned.1.call-start = ((), (), s32[]{:S(2)}) async-start(), calls=%async_computation.1 | async-start | bytes 8912896 | tf_op jit(solution)/shard_map/all_gather | solution.py:50
  7.3 298.6 %all-gather.5.cloned.1.call-start = ((), (), s32[]{:S(2)}) async-start(), calls=%async_computation.2 | async-start | bytes 8912896 | tf_op jit(solution)/shard_map/all_gather | solution.py:51
  8.0 644.8 %reduce-scatter.2.cloned.1.call-start = ((), (), s32[]{:S(2)}) async-start(), calls=%async_computation.3 | async-start | bytes 4456448 | tf_op jit(solution)/shard_map/reduce_scatter | solution.py:62
  305.9 4.5 copy-start.1
  307.9 6.5 copy-start
  321.4 4.5 copy-start.1
  323.4 6.5 copy-start
  339.1 4.5 copy-start.1
  341.1 6.5 copy-start
  356.8 4.5 copy-start.1
  358.7 6.5 copy-start
  374.5 4.5 copy-start.1
  376.4 6.5 copy-start
  392.2 4.5 copy-start.1
  394.1 6.5 copy-start
  409.8 4.5 copy-start.1
  411.8 6.5 copy-start
  427.5 4.5 copy-start.1
  429.5 6.5 copy-start
  445.2 4.5 copy-start.1
  447.2 6.5 copy-start
  462.9 4.5 copy-start.1
  464.9 6.5 copy-start
  480.6 4.5 copy-start.1
  482.6 6.5 copy-start
  498.3 4.5 copy-start.1
  500.3 6.5 copy-start
  516.0 4.5 copy-start.1
  517.9 6.5 copy-start
  533.7 4.5 copy-start.1
  535.6 6.5 copy-start
  551.4 4.5 copy-start.1
  553.3 6.5 copy-start
  569.0 4.5 copy-start.1
  571.0 6.5 copy-start
  653.8 8.7 %collective-permute-start = (f32[32,1024]{1,0:T(8,128)S(1)}, f32[32,1024]{1,0:T(8,128)S(1)}, u32[]{:S(2)}, u32[]{:S(2)}) collective-permute-start(f32[32,1024]{1,0:T(8,128)S(1)} %get-tuple-element.179), channel_id=1, source_target_pairs={{0,16},{16,32},{32,48},{48,64},{64,80},{80,96},{96,112},{112,128},... | collective-permute-start | bytes 393224 | tf_op jit(solution)/shard_map/ppermute | solution.py:12
Sparse Core Ops, SparseCore 0:
  9.8 149.1 all-gather.2
  161.5 144.3 all-gather.4
  586.9 65.8 reduce-scatter.1
where the time goes:
time: 675 us; the launch traced here: 670 us
  waiting for transfers between devices  372 us (55%)
  matrix products  154 us (23%)
  local copies, waits for them, and re-layouts  116 us (17%)
  between operations  13.8 us (2%)
  other arithmetic  11.6 us (2%)
    all_gather x1, waiting for transfers between devices, per_device(): occ_piece = lax.all_gather(green_occ, 'ao', axis=1, tiled=True)  150 us
    all_gather x1, waiting for transfers between devices, per_device(): vir_piece = lax.all_gather(green_virtual, 'ao', axis=1, tiled=True)  147 us
    dot_general x16, matrix products, pair_up(): lax.dot_general(occ_moment, vir_moment, (((0,), (0,)), ((), ())), preferr...  76 us
    convert_element_type x64, local copies, waits for them, and re-layouts, moment_rows(): moment.reshape(column_span * lam_rows, windows * block_size)  75 us
    reduce_scatter x1, waiting for transfers between devices, per_device(): summed = lax.psum_scatter(halves, 'pair', scatter_dimension=1, tiled=True)  66 us
    dot_general x32, matrix products, moment_rows(): jnp.einsum('csiq,cr->sirq', product, onehot, precision=lax.Precision.HIGH...  51.1 us
    dot_general x32, matrix products, moment_rows(): jnp.einsum('cjs,cjx->csx', picked_rows, tile_values, preferred_element_ty...  26.5 us
    dynamic_slice x16, local copies, waits for them, and re-layouts, step_shard(): vir_slice = lax.dynamic_slice_in_dim(vir_piece, offset, own_width, 1)  20.6 us
  transfers between devices with their start and end apart: 4, of which 4 were waited for; matrix products, arithmetic and copies ran while one was open for 0% of the time, Pallas kernels for 0%

commit v1 on v0

v1 whole, which is shorter than its diff:
```python
import functools

import jax
import jax.numpy as jnp
from jax import lax
from jax.experimental import pallas as pl
from jax.experimental.pallas import tpu as pltpu
from jax.sharding import PartitionSpec as P

AXES = ("ao", "pair")
BLK = 64
TILES = 16
PAIRS = TILES // 2
NAO = 2048
RW = 1024
COLS = 128
PIECE = NAO // 8
META = 16
BODY = PAIRS * 128
PAY = BODY + META
GROUPS = 8
DEPTH = GROUPS * 512
BF = jnp.bfloat16
F32 = jnp.float32


def device_of(index):
    ao, pair = index // 16, index % 16
    return ao // 8, ao % 8, pair // 4, (pair // 2) % 2, pair % 2


def index_of(x_hi, z, y, x_lo, core):
    return ((x_hi % 2) * 8 + z % 8) * 16 + ((y % 4) * 2 + x_lo % 2) * 2 + core % 2


def permute(value, where):
    pairs = [(source, index_of(*where(*device_of(source)))) for source in range(256)]
    return lax.ppermute(value, AXES, pairs)


def along_y(value, steps):
    return permute(value, lambda x_hi, z, y, x_lo, core: (x_hi, z, y + steps, x_lo, core))


def along_z(value, steps):
    return permute(value, lambda x_hi, z, y, x_lo, core: (x_hi, z + steps, y, x_lo, core))


def swap_x(value):
    return permute(value, lambda x_hi, z, y, x_lo, core: (x_hi, z, y, x_lo + 1, core))


def swap_core(value):
    return permute(value, lambda x_hi, z, y, x_lo, core: (x_hi, z, y, x_lo, core + 1))


def next_group(value, flip):
    def where(x_hi, z, y, x_lo, core):
        return (x_hi + (z == 7), z + 1, y, x_lo + flip, core)

    return permute(value, where)


Z_OFFSETS = ((3, 4), (1, 2), (0, 7), (5, 6))


def scatter_target(x_hi, z, y, x_lo, core):
    block = x_hi * 8 + z
    target_y, target_x, target_core = block // 4, (block // 2) % 2, block % 2
    target_hi = x_hi if x_lo == target_x else 1 - x_hi
    offset = Z_OFFSETS[(y - target_y) % 4][core]
    return target_hi, z + offset, target_y, target_x, target_core


def scatter_green(green_occ, green_virtual):
    table = jnp.array([scatter_target(*device_of(index))[1] % 8 for index in range(256)], jnp.int32)
    me = lax.axis_index("ao") * 16 + lax.axis_index("pair")
    start = table[me] * PIECE
    both = jnp.concatenate(
        [lax.dynamic_slice_in_dim(part, start, PIECE, 0) for part in (green_occ, green_virtual)], axis=1
    )
    return permute(both, scatter_target)


def pack_kernel(orbital_ref, window_ref, count_ref, tile_ref, out_ref, order_ref):
    live = count_ref[0]
    windows = [window_ref[slot] for slot in range(TILES)]
    keys = [
        jnp.where(slot < live, windows[slot], TILES) * TILES + slot for slot in range(TILES)
    ]
    ranks = [jnp.int32(0) for slot in range(TILES)]
    for first in range(TILES):
        for second in range(first + 1, TILES):
            later = (keys[second] < keys[first]).astype(jnp.int32)
            ranks[first] = ranks[first] + later
            ranks[second] = ranks[second] + (1 - later)
    for slot in range(TILES):
        order_ref[ranks[slot]] = slot
    lane = lax.broadcasted_iota(jnp.int32, (META, 128), 1)
    meta = jnp.where(lane == 32, live, jnp.zeros((META, 128), jnp.int32))
    last = jnp.int32(0)
    for slot in range(TILES):
        source = order_ref[slot]
        last = jnp.where(slot < live, window_ref[source], last)
        meta = jnp.where(lane == slot, last, meta)
        meta = jnp.where(lane == TILES + slot, orbital_ref[source], meta)
    for index in range(PAIRS):
        rows = []
        for slot in (2 * index, 2 * index + 1):
            rows.append(jnp.where(slot < live, tile_ref[order_ref[slot]].astype(F32), 0.0))
        both = jnp.concatenate(rows, axis=0)
        out_ref[pl.ds(index * 128, 128), :] = both.T.astype(BF)
    out_ref[pl.ds(BODY, META), :] = meta.astype(F32).astype(BF)


def pack(tile_orbital, tile_window, tile_count, tile_values):
    smem = pl.BlockSpec(memory_space=pltpu.SMEM)
    return pl.pallas_call(
        pack_kernel,
        out_shape=jax.ShapeDtypeStruct((PAY, 128), BF),
        in_specs=[smem, smem, smem, pl.BlockSpec(memory_space=pltpu.VMEM)],
        out_specs=pl.BlockSpec(memory_space=pltpu.VMEM),
        scratch_shapes=[pltpu.SMEM((TILES,), jnp.int32)],
    )(tile_orbital, tile_window, tile_count, tile_values)


def chi_kernel(
    place_ref, meta_ref, own_ref, east_ref, west_ref, far_a_ref, far_b_ref,
    green_ref, other_ref, keep_ref, send_ref, occ_ref, vir_ref, acc_ref,
):
    my_z, my_y, my_x, my_core = place_ref[0], place_ref[1], place_ref[2], place_ref[3]
    occ_ref[...] = jnp.zeros_like(occ_ref)
    vir_ref[...] = jnp.zeros_like(vir_ref)
    lane = lax.broadcasted_iota(jnp.int32, (128, 128), 1)

    def rows_of(orbital):
        piece = lax.rem(orbital // 4 - my_z + 8, 8)
        start = pl.multiple_of(piece * PIECE + lax.rem(orbital, 4) * BLK, BLK)
        return jnp.concatenate(
            [green_ref[pl.ds(start, BLK), :], other_ref[pl.ds(start, BLK), :]], axis=1
        )

    def group(tiles_ref, base, number):
        live = meta_ref[number, 2 * TILES]
        column = number * 512

        def step(index, carry):
            first, second = 2 * index, 2 * index + 1
            tile = tiles_ref[pl.ds(pl.multiple_of(base + index * 128, 16), 128), :]
            zero = jnp.zeros_like(tile)
            stacked = jnp.concatenate(
                [jnp.where(lane < BLK, tile, zero), jnp.where(lane < BLK, zero, tile)], axis=0
            )
            rows = jnp.concatenate(
                [rows_of(meta_ref[number, TILES + first]), rows_of(meta_ref[number, TILES + second])], axis=0
            )
            product = jnp.dot(stacked, rows, preferred_element_type=F32)
            windows = [meta_ref[number, first], meta_ref[number, second]]
            before = jnp.where(index > 0, meta_ref[number, jnp.maximum(first - 1, 0)], -1)
            total = product[:128]
            total = jnp.where(windows[0] == before, acc_ref[...] + total, total)
            store(total, windows[0])
            total = jnp.where(windows[1] == windows[0], total + product[128:], product[128:])
            acc_ref[...] = total
            store(total, windows[1])
            return carry

        def store(total, window):
            high, y, x = window // 8, lax.rem(window // 2, 4), lax.rem(window, 2)
            dy, dx = lax.rem(y - my_y + 4, 4), lax.rem(x - my_x + 2, 2)
            spot = ((dy * 2 + dx) * 2 + high) * 32
            vir_row = pl.multiple_of(window * BLK, BLK)
            half = total.astype(BF)
            for i in range(2):
                part = half[i * BLK:(i + 1) * BLK]
                occ = jnp.concatenate([part[:, 0:128], part[:, 256:384]], axis=1)
                vir = jnp.concatenate([part[:, 128:256], part[:, 384:512]], axis=1)
                vir_ref[pl.ds(vir_row, BLK), pl.ds(column + i * 256, 256)] = vir
                for core in range(2):
                    row = jnp.where(my_core == core, 0, 512) + spot
                    row = pl.multiple_of(row, 32)
                    occ_ref[pl.ds(row, 32), pl.ds(column + i * 256, 256)] = occ[core * 32:(core + 1) * 32]

        lax.fori_loop(0, lax.div(live + 1, 2), step, 0)

    number = 0
    for tiles_ref in (own_ref, east_ref, west_ref, far_a_ref, far_b_ref):
        for base in range(0, tiles_ref.shape[0], PAY):
            group(tiles_ref, base, number)
            number += 1

    def chi(row, target_ref, kind):
        for m in range(0, 512, 256):
            @pl.loop(0, RW, step=256)
            def _(n):
                n = pl.multiple_of(n, 256)
                product = lax.dot_general(
                    occ_ref[pl.ds(row + m, 256), :], vir_ref[pl.ds(n, 256), :],
                    (((1,), (1,)), ((), ())), preferred_element_type=F32,
                )
                target_ref[pl.ds(m, 256), pl.ds(n, 256)] = product.astype(kind)

    chi(512, send_ref, BF)
    chi(0, keep_ref, F32)


def chi_call(place, meta, tiles, green, other):
    smem = pl.BlockSpec(memory_space=pltpu.SMEM)
    vmem = pl.BlockSpec(memory_space=pltpu.VMEM)
    return pl.pallas_call(
        chi_kernel,
        out_shape=(jax.ShapeDtypeStruct((512, RW), F32), jax.ShapeDtypeStruct((512, RW), BF)),
        in_specs=[smem, smem] + [vmem] * 7,
        out_specs=(vmem, vmem),
        scratch_shapes=[
            pltpu.VMEM((RW, DEPTH), BF),
            pltpu.VMEM((RW, DEPTH), BF),
            pltpu.VMEM((128, 512), F32),
        ],
        compiler_params=pltpu.CompilerParams(vmem_limit_bytes=48 * 1024 * 1024),
        cost_estimate=pl.CostEstimate(flops=12 * 10**9, bytes_accessed=8 * 2**20, transcendentals=0),
    )(place, meta, *tiles, green, other)


def gather_tiles(payload):
    own = jnp.concatenate([payload, swap_x(payload)], axis=0)
    east = along_y(own, 1)
    west = along_y(own, -1)
    far_a = along_y(east[:PAY], 1)
    far_b = along_y(west[PAY:], -1)
    return own, east, west, far_a, far_b


def gather_green(piece):
    up, down = piece, piece
    ups, downs = [], []
    for unused in range(3):
        up = along_z(up, 1)
        down = along_z(down, -1)
        ups.append(up)
        downs.append(down)
    half = PIECE // 2
    across = [along_z(up[:half], 1), along_z(down[half:], -1)]
    return jnp.concatenate([piece] + downs + across + ups[::-1], axis=0)


def reduce_band(keep, send):
    quarters = (keep + swap_core(send).astype(F32)).astype(F32).reshape(4, 128, RW)
    ahead = along_y(quarters[2, :64].astype(BF), 1).astype(F32)
    behind = along_y(quarters[2, 64:].astype(BF), -1).astype(F32)
    up = jnp.concatenate([quarters[1, :64] + ahead, quarters[1, 64:]], axis=0).astype(BF)
    down = jnp.concatenate([quarters[3, :64], quarters[3, 64:] + behind], axis=0).astype(BF)
    total = quarters[0] + along_y(up, 1).astype(F32) + along_y(down, -1).astype(F32)
    upper = total[:32] + swap_x(total[64:96].astype(BF)).astype(F32)
    lower = next_group(total[32:64].astype(BF), 0).astype(F32) + next_group(total[96:].astype(BF), 1).astype(F32)
    return jnp.concatenate([lower[:, :512], lower[:, 512:] + upper[:, :512], upper[:, 512:]], axis=1)


def per_device(green_occ, green_virtual, tile_values, tile_orbital, tile_window, tile_count):
    ao, pair = lax.axis_index("ao"), lax.axis_index("pair")
    place = jnp.stack([ao % 8, pair // 4, (pair // 2) % 2, pair % 2]).astype(jnp.int32)
    piece = scatter_green(green_occ, green_virtual)
    payload = pack(tile_orbital, tile_window, tile_count, tile_values)
    tiles = gather_tiles(payload)
    green = gather_green(piece)
    other = swap_core(green)
    rows = [part[start + BODY:start + BODY + 1, :64] for part in tiles for start in range(0, part.shape[0], PAY)]
    meta = jnp.concatenate(rows, axis=0).astype(jnp.int32)
    keep, send = chi_call(place, meta, tiles, green, other)
    return reduce_band(keep, send)


def solution(mesh):
    in_specs = (
        P(None, "ao"),
        P(None, "ao"),
        P(("ao", "pair"), None, None),
        P(("ao", "pair")),
        P(("ao", "pair")),
        P(("ao", "pair")),
    )
    out_specs = P(("ao", "pair"), None)
    return jax.shard_map(
        per_device, mesh=mesh, in_specs=in_specs, out_specs=out_specs, check_vma=False
    )
```

time: 675 us -> 133 us (0.20)
  waiting for transfers between devices: 372 us -> 60.1 us
  matrix products: 154 us -> 0 us
  local copies, waits for them, and re-layouts: 116 us -> 2.38 us
  starting transfers between devices: 1.63 us -> 39.8 us
  Pallas kernels: 0 us -> 24.8 us
  between operations: 13.8 us -> 1.57 us
  other arithmetic: 11.6 us -> 3.14 us
    all_gather x2 -> x0, waiting for transfers between devices: 297 us -> none  [the longest x1 150 us: per_device(): occ_piece = lax.all_gather(green_occ, 'ao', axis=1, tiled=True)]
    dot_general x80 -> x0, matrix products: 154 us -> none  [the longest x16 76 us: pair_up(): lax.dot_general(occ_moment, vir_moment, (((0,), (0,)), ((), ())), preferr...]
    convert_element_type x64 -> x1, local copies, waits for them, and re-layouts: 75 us -> 0.04 us  [reduce_band(): ahead = along_y(quarters[2, :64].astype(BF), 1).astype(F32)]
    reduce_scatter x1 -> x0, waiting for transfers between devices: 66 us -> none  [per_device(): summed = lax.psum_scatter(halves, 'pair', scatter_dimension=1, tiled=True)]
    ppermute x1 -> x23, waiting for transfers between devices: 7.1 us -> 60.1 us  [permute(): return lax.ppermute(value, AXES, pairs)]
    ppermute x1 -> x23, starting transfers between devices: 1.55 us -> 39.8 us  [permute(): return lax.ppermute(value, AXES, pairs)]
    pallas_call x0 -> x2, Pallas kernels: none -> 24.8 us  [the longest x1 22.7 us: chi_call(): pl.pallas_call(chi_kernel, out_shape=(jax.ShapeDtypeStruct((512, RW), F32...]
    gather x32 -> x0, local copies, waits for them, and re-layouts: 19.1 us -> none  [moment_rows(): green_part.reshape(orbitals // block_size, block_size, column_span)]
  transfers between devices with their start and end apart: 4 -> 23, of which waited for: 4 -> 13; matrix products, arithmetic and copies ran while one was open for 0% -> 0% of each run, Pallas kernels for 0% -> 2%
where the time goes in v1:
time: 133 us; the launch traced here: 132 us
  waiting for transfers between devices  60.1 us (45%)
  starting transfers between devices  39.8 us (30%)
  Pallas kernels  24.8 us (19%)
  other arithmetic  3.14 us (2%)
  local copies, waits for them, and re-layouts  2.38 us (2%)
  between operations  1.57 us (1%)
    ppermute x23, waiting for transfers between devices, permute(): return lax.ppermute(value, AXES, pairs)  60.1 us
    ppermute x23, starting transfers between devices, permute(): return lax.ppermute(value, AXES, pairs)  39.8 us
    pallas_call x1, Pallas kernels, chi_call(): pl.pallas_call(chi_kernel, out_shape=(jax.ShapeDtypeStruct((512, RW), F32...  22.7 us
  transfers between devices with their start and end apart: 23, of which 13 were waited for; matrix products, arithmetic and copies ran while one was open for 0% of the time, Pallas kernels for 2%

profile of v1, /device:TPU:6, one launch (start us, length us, event | category | flops | bytes accessed | tf_op | source)
XLA Modules:
  0.0 131.8 jit_solution(4365284491768406968)
XLA Ops:
  0.0 1.3 dynamic_slice.9
  1.9 0.9 constant_dynamic-slice_fusion
  2.8 3.2 %collective-permute-start.5 = (bf16[256,256]{1,0:T(8,128)(2,1)S(1)}, bf16[256,256]{1,0:T(8,128)(2,1)S(1)}, u32[]{:S(2)}, u32[]{:S(2)}) collective-permute-start(bf16[256,256]{1,0:T(8,128)(2,1)S(1)} %pad_maximum_fusion.4), channel_id=1, source_target_pairs={{0,48},{1,64},{2,176},{3,192},{4,16},{5,32},{6,144},{7,160},{8,0},... | collective-permute-start | bytes 393224 | tf_op jit(solution)/shard_map/ppermute | solution.py:38
  6.0 9.3 %collective-permute-done.5 = bf16[256,256]{1,0:T(8,128)(2,1)S(1)} collective-permute-done((bf16[256,256]{1,0:T(8,128)(2,1)S(1)}, bf16[256,256]{1,0:T(8,128)(2,1)S(1)}, u32[]{:S(2)}, u32[]{:S(2)}) %collective-permute-start.5) | collective-permute-done | bytes 131104 | tf_op jit(solution)/shard_map/ppermute | solution.py:38
  15.3 0.0 collective-permute-start.9
  15.3 5.7 %collective-permute-start.6 = (bf16[256,256]{1,0:T(8,128)(2,1)S(1)}, bf16[256,256]{1,0:T(8,128)(2,1)S(1)}, u32[]{:S(2)}, u32[]{:S(2)}) collective-permute-start(bf16[256,256]{1,0:T(8,128)(2,1)S(1)} %collective-permute-done.5), channel_id=1, source_target_pairs={{0,112},{1,113},{2,114},{3,115},{4,116},{5,117},{6,118},{7,119},{8... | collective-permute-start | bytes 393224 | tf_op jit(solution)/shard_map/ppermute | solution.py:38
  21.1 3.7 %collective-permute-done.9 = bf16[256,256]{1,0:T(8,128)(2,1)S(1)} collective-permute-done((bf16[256,256]{1,0:T(8,128)(2,1)S(1)}, bf16[256,256]{1,0:T(8,128)(2,1)S(1)}, u32[]{:S(2)}, u32[]{:S(2)}) %collective-permute-start.9) | collective-permute-done | bytes 131104 | tf_op jit(solution)/shard_map/ppermute | solution.py:38
  24.8 0.0 collective-permute-start.10
  24.8 0.0 collective-permute-done.6
  24.8 3.2 %collective-permute-start.7 = (bf16[256,256]{1,0:T(8,128)(2,1)S(1)}, bf16[256,256]{1,0:T(8,128)(2,1)S(1)}, u32[]{:S(2)}, u32[]{:S(2)}) collective-permute-start(bf16[256,256]{1,0:T(8,128)(2,1)S(1)} %collective-permute-done.6), channel_id=1, source_target_pairs={{0,112},{1,113},{2,114},{3,115},{4,116},{5,117},{6,118},{7,119},{8... | collective-permute-start | bytes 393224 | tf_op jit(solution)/shard_map/ppermute | solution.py:38
  28.7 2.1 %shard_map.73 = bf16[1040,128]{1,0:T(8,128)(2,1)} custom-call(s32[16]{0:T(128)} %orbital_ref.1, s32[16]{0:T(128)} %window_ref.1, s32[1]{0:T(128)S(6)} %copy.16.count_ref, bf16[16,64,128]{2,1,0:T(8,128)(2,1)} %tile_ref.1), custom_call_target="tpu_custom_call" | custom-call | tf_op jit(solution)/shard_map/pallas_call | solution.py:118
  30.7 0.0 copy-start
  30.7 1.3 collective-permute-start
  32.0 0.0 collective-permute-done.10
  32.0 0.1 collective-permute-start.11
  32.1 0.0 collective-permute-done.7
  32.2 3.2 %collective-permute-start.8 = (bf16[256,256]{1,0:T(8,128)(2,1)S(1)}, bf16[256,256]{1,0:T(8,128)(2,1)S(1)}, u32[]{:S(2)}, u32[]{:S(2)}) collective-permute-start(bf16[256,256]{1,0:T(8,128)(2,1)S(1)} %collective-permute-done.7), channel_id=1, source_target_pairs={{0,112},{1,113},{2,114},{3,115},{4,116},{5,117},{6,118},{7,119},{8... | collective-permute-start | bytes 393224 | tf_op jit(solution)/shard_map/ppermute | solution.py:38
  35.4 2.9 %collective-permute-done.11 = bf16[256,256]{1,0:T(8,128)(2,1)S(1)} collective-permute-done((bf16[256,256]{1,0:T(8,128)(2,1)S(1)}, bf16[256,256]{1,0:T(8,128)(2,1)S(1)}, u32[]{:S(2)}, u32[]{:S(2)}) %collective-permute-start.11) | collective-permute-done | bytes 131104 | tf_op jit(solution)/shard_map/ppermute | solution.py:38
  38.3 0.0 collective-permute-start.12
  38.3 0.0 collective-permute-done.8
  38.3 3.3 %collective-permute-start.13 = (bf16[128,256]{1,0:T(8,128)(2,1)S(1)}, bf16[128,256]{1,0:T(8,128)(2,1)S(1)}, u32[]{:S(2)}, u32[]{:S(2)}) collective-permute-start(bf16[128,256]{1,0:T(8,128)(2,1)S(1)} %slice.127), channel_id=1, source_target_pairs={{0,112},{1,113},{2,114},{3,115},{4,116},{5,117},{6,118},{7,119},{8... | collective-permute-start | bytes 196616 | tf_op jit(solution)/shard_map/ppermute | solution.py:38
  41.6 2.1 %collective-permute-done.12 = bf16[128,256]{1,0:T(8,128)(2,1)S(1)} collective-permute-done((bf16[128,256]{1,0:T(8,128)(2,1)S(1)}, bf16[128,256]{1,0:T(8,128)(2,1)S(1)}, u32[]{:S(2)}, u32[]{:S(2)}) %collective-permute-start.12) | collective-permute-done | bytes 65568 | tf_op jit(solution)/shard_map/ppermute | solution.py:38
  43.8 0.0 collective-permute-done.13
  43.9 0.1 collective-permute-start.14
  44.0 0.0 collective-permute-done
  44.0 0.0 copy-done
  44.0 0.4 collective-permute-start.2
  44.5 1.7 %collective-permute-start.1 = (bf16[2080,128]{1,0:T(8,128)(2,1)S(1)}, bf16[2080,128]{1,0:T(8,128)(2,1)S(1)}, u32[]{:S(2)}, u32[]{:S(2)}) collective-permute-start(bf16[2080,128]{1,0:T(8,128)(2,1)S(1)} %pad_maximum_fusion.own_ref), channel_id=1, source_target_pairs={{0,4},{1,5},{2,6},{3,7},{4,8},{5,9},{6,10},{7,11},{8,12},{9,13},{1... | collective-permute-start | bytes 1597448 | tf_op jit(solution)/shard_map/ppermute | solution.py:38
  46.1 0.1 pad_add_fusion.place_ref
  46.2 12.4 %collective-permute-done.2.west_ref = bf16[2080,128]{1,0:T(8,128)(2,1)S(1)} collective-permute-done((bf16[2080,128]{1,0:T(8,128)(2,1)S(1)}, bf16[2080,128]{1,0:T(8,128)(2,1)S(1)}, u32[]{:S(2)}, u32[]{:S(2)}) %collective-permute-start.2) | collective-permute-done | bytes 532512 | tf_op jit(solution)/shard_map/ppermute | solution.py:38
  58.6 1.7 %collective-permute-start.4 = (bf16[1040,128]{1,0:T(8,128)(2,1)S(1)}, bf16[1040,128]{1,0:T(8,128)(2,1)S(1)}, u32[]{:S(2)}, u32[]{:S(2)}) collective-permute-start(bf16[1040,128]{1,0:T(8,128)(2,1)S(1)} %slice.124), channel_id=1, source_target_pairs={{0,12},{1,13},{2,14},{3,15},{4,0},{5,1},{6,2},{7,3},{8,4},{9,5},{1... | collective-permute-start | bytes 798728 | tf_op jit(solution)/shard_map/ppermute | solution.py:38
  60.3 0.0 collective-permute-done.1.east_ref
  60.3 0.7 collective-permute-start.3
  61.0 5.7 %collective-permute-done.4.far_b_ref = bf16[1040,128]{1,0:T(8,128)(2,1)S(1)} collective-permute-done((bf16[1040,128]{1,0:T(8,128)(2,1)S(1)}, bf16[1040,128]{1,0:T(8,128)(2,1)S(1)}, u32[]{:S(2)}, u32[]{:S(2)}) %collective-permute-start.4) | collective-permute-done | bytes 266272 | tf_op jit(solution)/shard_map/ppermute | solution.py:38
  66.7 2.8 %collective-permute-done.3.far_a_ref = bf16[1040,128]{1,0:T(8,128)(2,1)S(1)} collective-permute-done((bf16[1040,128]{1,0:T(8,128)(2,1)S(1)}, bf16[1040,128]{1,0:T(8,128)(2,1)S(1)}, u32[]{:S(2)}, u32[]{:S(2)}) %collective-permute-start.3) | collective-permute-done | bytes 266272 | tf_op jit(solution)/shard_map/ppermute | solution.py:38
  69.5 0.0 collective-permute-done.14.other_ref
  69.5 22.7 %shard_map.74 = (f32[512,1024]{1,0:T(8,128)}, bf16[512,1024]{1,0:T(8,128)(2,1)S(1)}) custom-call(s32[4]{0:T(128)S(1)} %pad_add_fusion.place_ref, s32[8,64]{1,0:T(8,128)S(1)} %convert_element_type.40.meta_ref, bf16[2080,128]{1,0:T(8,128)(2,1)S(1)} %pad_maximum_fusion.own_ref, bf16[2080,128]{1,0:T(8,128)(2,1)S(1)} %collective-permute-done.1.east_ref, ...), custom_call_target="tpu_custom_call" | custom-call | flops 12000000000 | bytes 8388608 | tf_op jit(solution)/shard_map/pallas_call | solution.py:210
  92.3 0.0 collective-permute-start.15
  92.3 2.7 %collective-permute-done.15 = bf16[512,1024]{1,0:T(8,128)(2,1)S(1)} collective-permute-done((bf16[512,1024]{1,0:T(8,128)(2,1)S(1)}, bf16[512,1024]{1,0:T(8,128)(2,1)S(1)}, u32[]{:S(2)}, u32[]{:S(2)}) %collective-permute-start.15) | collective-permute-done | bytes 1048608 | tf_op jit(solution)/shard_map/ppermute | solution.py:38
  94.9 1.9 %convert_add_fusion = f32[512,1024]{1,0:T(8,128)S(1)} fusion(f32[512,1024]{1,0:T(8,128)} %get-tuple-element.7, bf16[512,1024]{1,0:T(8,128)(2,1)S(1)} %collective-permute-done.15), kind=kLoop, calls=%fused_computation | loop fusion | flops 1048576 | bytes 5242880 | tf_op jit(solution)/shard_map/add | solution.py:248
  96.8 0.2 convert.21
  97.0 0.1 collective-permute-start.16
  97.1 3.2 %collective-permute-start.18 = (bf16[64,1024]{1,0:T(8,128)(2,1)S(1)}, bf16[64,1024]{1,0:T(8,128)(2,1)S(1)}, u32[]{:S(2)}, u32[]{:S(2)}) collective-permute-start(bf16[64,1024]{1,0:T(8,128)(2,1)S(1)} %get-tuple-element.14), channel_id=1, source_target_pairs={{0,12},{1,13},{2,14},{3,15},{4,0},{5,1},{6,2},{7,3},{8,4},{9,5},{1... | collective-permute-start | bytes 393224 | tf_op jit(solution)/shard_map/ppermute | solution.py:38
  100.3 3.5 %collective-permute-done.16 = bf16[64,1024]{1,0:T(8,128)(2,1)S(1)} collective-permute-done((bf16[64,1024]{1,0:T(8,128)(2,1)S(1)}, bf16[64,1024]{1,0:T(8,128)(2,1)S(1)}, u32[]{:S(2)}, u32[]{:S(2)}) %collective-permute-start.16) | collective-permute-done | bytes 131104 | tf_op jit(solution)/shard_map/ppermute | solution.py:38
  103.9 0.0 collective-permute-done.18
  103.9 0.1 fusion.4
  104.0 3.0 %collective-permute-start.19 = (bf16[128,1024]{1,0:T(8,128)(2,1)S(1)}, bf16[128,1024]{1,0:T(8,128)(2,1)S(1)}, u32[]{:S(2)}, u32[]{:S(2)}) collective-permute-start(bf16[128,1024]{1,0:T(8,128)(2,1)S(1)} %pad_maximum_fusion.2), channel_id=1, source_target_pairs={{0,12},{1,13},{2,14},{3,15},{4,0},{5,1},{6,2},{7,3},{8,4},{9,5},{1... | collective-permute-start | bytes 786440 | tf_op jit(solution)/shard_map/ppermute | solution.py:38
  107.0 0.1 collective-permute-start.17
  107.1 4.6 %collective-permute-done.19 = bf16[128,1024]{1,0:T(8,128)(2,1)S(1)} collective-permute-done((bf16[128,1024]{1,0:T(8,128)(2,1)S(1)}, bf16[128,1024]{1,0:T(8,128)(2,1)S(1)}, u32[]{:S(2)}, u32[]{:S(2)}) %collective-permute-start.19) | collective-permute-done | bytes 262176 | tf_op jit(solution)/shard_map/ppermute | solution.py:38
  111.7 3.5 %collective-permute-done.17 = bf16[128,1024]{1,0:T(8,128)(2,1)S(1)} collective-permute-done((bf16[128,1024]{1,0:T(8,128)(2,1)S(1)}, bf16[128,1024]{1,0:T(8,128)(2,1)S(1)}, u32[]{:S(2)}, u32[]{:S(2)}) %collective-permute-start.17) | collective-permute-done | bytes 262176 | tf_op jit(solution)/shard_map/ppermute | solution.py:38
  115.2 0.1 fusion.5
  115.4 2.3 %collective-permute-start.22 = (bf16[32,1024]{1,0:T(8,128)(2,1)S(1)}, bf16[32,1024]{1,0:T(8,128)(2,1)S(1)}, u32[]{:S(2)}, u32[]{:S(2)}) collective-permute-start(bf16[32,1024]{1,0:T(8,128)(2,1)S(1)} %get-tuple-element.22), channel_id=1, source_target_pairs={{0,2},{1,3},{2,0},{3,1},{4,6},{5,7},{6,4},{7,5},{8,10},{9,11},{10,... | collective-permute-start | bytes 196616 | tf_op jit(solution)/shard_map/ppermute | solution.py:38
  117.6 5.8 %collective-permute-start.20 = (bf16[32,1024]{1,0:T(8,128)(2,1)S(1)}, bf16[32,1024]{1,0:T(8,128)(2,1)S(1)}, u32[]{:S(2)}, u32[]{:S(2)}) collective-permute-start(bf16[32,1024]{1,0:T(8,128)(2,1)S(1)} %get-tuple-element.21), channel_id=1, source_target_pairs={{0,16},{1,17},{2,18},{3,19},{4,20},{5,21},{6,22},{7,23},{8,24},{9,... | collective-permute-start | bytes 196616 | tf_op jit(solution)/shard_map/ppermute | solution.py:38
  123.5 0.7 collective-permute-start.21
  124.2 0.0 collective-permute-done.22
  124.2 1.3 %collective-permute-done.20 = bf16[32,1024]{1,0:T(8,128)(2,1)S(1)} collective-permute-done((bf16[32,1024]{1,0:T(8,128)(2,1)S(1)}, bf16[32,1024]{1,0:T(8,128)(2,1)S(1)}, u32[]{:S(2)}, u32[]{:S(2)}) %collective-permute-start.20) | collective-permute-done | bytes 65568 | tf_op jit(solution)/shard_map/ppermute | solution.py:38
  125.5 5.5 %collective-permute-done.21 = bf16[32,1024]{1,0:T(8,128)(2,1)S(1)} collective-permute-done((bf16[32,1024]{1,0:T(8,128)(2,1)S(1)}, bf16[32,1024]{1,0:T(8,128)(2,1)S(1)}, u32[]{:S(2)}, u32[]{:S(2)}) %collective-permute-start.21) | collective-permute-done | bytes 65568 | tf_op jit(solution)/shard_map/ppermute | solution.py:38
  131.1 0.7 pad_maximum_fusion.3
  (30 shorter events, 0.4 us)
Async XLA Ops:
  2.8 12.5 %collective-permute-start.5 = (bf16[256,256]{1,0:T(8,128)(2,1)S(1)}, bf16[256,256]{1,0:T(8,128)(2,1)S(1)}, u32[]{:S(2)}, u32[]{:S(2)}) collective-permute-start(bf16[256,256]{1,0:T(8,128)(2,1)S(1)} %pad_maximum_fusion.4), channel_id=1, source_target_pairs={{0,48},{1,64},{2,176},{3,192},{4,16},{5,32},{6,144},{7,160},{8,0},... | collective-permute-start | bytes 393224 | tf_op jit(solution)/shard_map/ppermute | solution.py:38
  15.3 9.4 %collective-permute-start.9 = (bf16[256,256]{1,0:T(8,128)(2,1)S(1)}, bf16[256,256]{1,0:T(8,128)(2,1)S(1)}, u32[]{:S(2)}, u32[]{:S(2)}) collective-permute-start(bf16[256,256]{1,0:T(8,128)(2,1)S(1)} %collective-permute-done.5), channel_id=1, source_target_pairs={{0,16},{1,17},{2,18},{3,19},{4,20},{5,21},{6,22},{7,23},{8,24},{9,... | collective-permute-start | bytes 393224 | tf_op jit(solution)/shard_map/ppermute | solution.py:38
  15.3 9.4 %collective-permute-start.6 = (bf16[256,256]{1,0:T(8,128)(2,1)S(1)}, bf16[256,256]{1,0:T(8,128)(2,1)S(1)}, u32[]{:S(2)}, u32[]{:S(2)}) collective-permute-start(bf16[256,256]{1,0:T(8,128)(2,1)S(1)} %collective-permute-done.5), channel_id=1, source_target_pairs={{0,112},{1,113},{2,114},{3,115},{4,116},{5,117},{6,118},{7,119},{8... | collective-permute-start | bytes 393224 | tf_op jit(solution)/shard_map/ppermute | solution.py:38
  24.8 7.3 %collective-permute-start.10 = (bf16[256,256]{1,0:T(8,128)(2,1)S(1)}, bf16[256,256]{1,0:T(8,128)(2,1)S(1)}, u32[]{:S(2)}, u32[]{:S(2)}) collective-permute-start(bf16[256,256]{1,0:T(8,128)(2,1)S(1)} %collective-permute-done.9), channel_id=1, source_target_pairs={{0,16},{1,17},{2,18},{3,19},{4,20},{5,21},{6,22},{7,23},{8,24},{9,... | collective-permute-start | bytes 393224 | tf_op jit(solution)/shard_map/ppermute | solution.py:38
  24.8 7.4 %collective-permute-start.7 = (bf16[256,256]{1,0:T(8,128)(2,1)S(1)}, bf16[256,256]{1,0:T(8,128)(2,1)S(1)}, u32[]{:S(2)}, u32[]{:S(2)}) collective-permute-start(bf16[256,256]{1,0:T(8,128)(2,1)S(1)} %collective-permute-done.6), channel_id=1, source_target_pairs={{0,112},{1,113},{2,114},{3,115},{4,116},{5,117},{6,118},{7,119},{8... | collective-permute-start | bytes 393224 | tf_op jit(solution)/shard_map/ppermute | solution.py:38
  30.7 13.3 %copy-start = (bf16[1040,128]{1,0:T(8,128)(2,1)S(1)}, bf16[1040,128]{1,0:T(8,128)(2,1)}, u32[]{:S(2)}) copy-start(bf16[1040,128]{1,0:T(8,128)(2,1)} %shard_map.73) | copy-start | bytes 798724
  30.7 13.2 %collective-permute-start = (bf16[1040,128]{1,0:T(8,128)(2,1)}, bf16[1040,128]{1,0:T(8,128)(2,1)S(1)}, u32[]{:S(2)}, u32[]{:S(2)}) collective-permute-start(bf16[1040,128]{1,0:T(8,128)(2,1)} %shard_map.73), channel_id=1, source_target_pairs={{0,2},{1,3},{2,0},{3,1},{4,6},{5,7},{6,4},{7,5},{8,10},{9,11},{10,... | collective-permute-start | bytes 798728 | tf_op jit(solution)/shard_map/ppermute | solution.py:38
  32.0 6.3 %collective-permute-start.11 = (bf16[256,256]{1,0:T(8,128)(2,1)S(1)}, bf16[256,256]{1,0:T(8,128)(2,1)S(1)}, u32[]{:S(2)}, u32[]{:S(2)}) collective-permute-start(bf16[256,256]{1,0:T(8,128)(2,1)S(1)} %collective-permute-done.10), channel_id=1, source_target_pairs={{0,16},{1,17},{2,18},{3,19},{4,20},{5,21},{6,22},{7,23},{8,24},{9,... | collective-permute-start | bytes 393224 | tf_op jit(solution)/shard_map/ppermute | solution.py:38
  32.2 6.2 %collective-permute-start.8 = (bf16[256,256]{1,0:T(8,128)(2,1)S(1)}, bf16[256,256]{1,0:T(8,128)(2,1)S(1)}, u32[]{:S(2)}, u32[]{:S(2)}) collective-permute-start(bf16[256,256]{1,0:T(8,128)(2,1)S(1)} %collective-permute-done.7), channel_id=1, source_target_pairs={{0,112},{1,113},{2,114},{3,115},{4,116},{5,117},{6,118},{7,119},{8... | collective-permute-start | bytes 393224 | tf_op jit(solution)/shard_map/ppermute | solution.py:38
  38.3 5.5 %collective-permute-start.12 = (bf16[128,256]{1,0:T(8,128)(2,1)S(1)}, bf16[128,256]{1,0:T(8,128)(2,1)S(1)}, u32[]{:S(2)}, u32[]{:S(2)}) collective-permute-start(bf16[128,256]{1,0:T(8,128)(2,1)S(1)} %slice.126), channel_id=1, source_target_pairs={{0,16},{1,17},{2,18},{3,19},{4,20},{5,21},{6,22},{7,23},{8,24},{9,... | collective-permute-start | bytes 196616 | tf_op jit(solution)/shard_map/ppermute | solution.py:38
  38.3 5.5 %collective-permute-start.13 = (bf16[128,256]{1,0:T(8,128)(2,1)S(1)}, bf16[128,256]{1,0:T(8,128)(2,1)S(1)}, u32[]{:S(2)}, u32[]{:S(2)}) collective-permute-start(bf16[128,256]{1,0:T(8,128)(2,1)S(1)} %slice.127), channel_id=1, source_target_pairs={{0,112},{1,113},{2,114},{3,115},{4,116},{5,117},{6,118},{7,119},{8... | collective-permute-start | bytes 196616 | tf_op jit(solution)/shard_map/ppermute | solution.py:38
  43.9 25.7 %collective-permute-start.14 = (bf16[2048,256]{1,0:T(8,128)(2,1)S(1)}, bf16[2048,256]{1,0:T(8,128)(2,1)}, u32[]{:S(2)}, u32[]{:S(2)}) collective-permute-start(bf16[2048,256]{1,0:T(8,128)(2,1)S(1)} %constant_dynamic-update-slice_fusion.green_ref), channel_id=1, source_target_pairs={{0,1},{1,0},{2,3},{3,2},{4,5},{5,4},{6,7},{7,6},{8,9},{9,8},{10,11... | collective-permute-start | bytes 3145736 | tf_op jit(solution)/shard_map/ppermute | solution.py:38
  44.0 14.6 %collective-permute-start.2 = (bf16[2080,128]{1,0:T(8,128)(2,1)S(1)}, bf16[2080,128]{1,0:T(8,128)(2,1)S(1)}, u32[]{:S(2)}, u32[]{:S(2)}) collective-permute-start(bf16[2080,128]{1,0:T(8,128)(2,1)S(1)} %pad_maximum_fusion.own_ref), channel_id=1, source_target_pairs={{0,12},{1,13},{2,14},{3,15},{4,0},{5,1},{6,2},{7,3},{8,4},{9,5},{1... | collective-permute-start | bytes 1597448 | tf_op jit(solution)/shard_map/ppermute | solution.py:38
  44.5 15.8 %collective-permute-start.1 = (bf16[2080,128]{1,0:T(8,128)(2,1)S(1)}, bf16[2080,128]{1,0:T(8,128)(2,1)S(1)}, u32[]{:S(2)}, u32[]{:S(2)}) collective-permute-start(bf16[2080,128]{1,0:T(8,128)(2,1)S(1)} %pad_maximum_fusion.own_ref), channel_id=1, source_target_pairs={{0,4},{1,5},{2,6},{3,7},{4,8},{5,9},{6,10},{7,11},{8,12},{9,13},{1... | collective-permute-start | bytes 1597448 | tf_op jit(solution)/shard_map/ppermute | solution.py:38
  58.6 8.1 %collective-permute-start.4 = (bf16[1040,128]{1,0:T(8,128)(2,1)S(1)}, bf16[1040,128]{1,0:T(8,128)(2,1)S(1)}, u32[]{:S(2)}, u32[]{:S(2)}) collective-permute-start(bf16[1040,128]{1,0:T(8,128)(2,1)S(1)} %slice.124), channel_id=1, source_target_pairs={{0,12},{1,13},{2,14},{3,15},{4,0},{5,1},{6,2},{7,3},{8,4},{9,5},{1... | collective-permute-start | bytes 798728 | tf_op jit(solution)/shard_map/ppermute | solution.py:38
  60.3 9.2 %collective-permute-start.3 = (bf16[1040,128]{1,0:T(8,128)(2,1)S(1)}, bf16[1040,128]{1,0:T(8,128)(2,1)S(1)}, u32[]{:S(2)}, u32[]{:S(2)}) collective-permute-start(bf16[1040,128]{1,0:T(8,128)(2,1)S(1)} %slice.122), channel_id=1, source_target_pairs={{0,4},{1,5},{2,6},{3,7},{4,8},{5,9},{6,10},{7,11},{8,12},{9,13},{1... | collective-permute-start | bytes 798728 | tf_op jit(solution)/shard_map/ppermute | solution.py:38
  92.3 2.7 %collective-permute-start.15 = (bf16[512,1024]{1,0:T(8,128)(2,1)S(1)}, bf16[512,1024]{1,0:T(8,128)(2,1)S(1)}, u32[]{:S(2)}, u32[]{:S(2)}) collective-permute-start(bf16[512,1024]{1,0:T(8,128)(2,1)S(1)} %get-tuple-element.8), channel_id=1, source_target_pairs={{0,1},{1,0},{2,3},{3,2},{4,5},{5,4},{6,7},{7,6},{8,9},{9,8},{10,11... | collective-permute-start | bytes 3145736 | tf_op jit(solution)/shard_map/ppermute | solution.py:38
  97.0 6.8 %collective-permute-start.16 = (bf16[64,1024]{1,0:T(8,128)(2,1)S(1)}, bf16[64,1024]{1,0:T(8,128)(2,1)S(1)}, u32[]{:S(2)}, u32[]{:S(2)}) collective-permute-start(bf16[64,1024]{1,0:T(8,128)(2,1)S(1)} %get-tuple-element.13), channel_id=1, source_target_pairs={{0,4},{1,5},{2,6},{3,7},{4,8},{5,9},{6,10},{7,11},{8,12},{9,13},{1... | collective-permute-start | bytes 393224 | tf_op jit(solution)/shard_map/ppermute | solution.py:38
  97.1 6.7 %collective-permute-start.18 = (bf16[64,1024]{1,0:T(8,128)(2,1)S(1)}, bf16[64,1024]{1,0:T(8,128)(2,1)S(1)}, u32[]{:S(2)}, u32[]{:S(2)}) collective-permute-start(bf16[64,1024]{1,0:T(8,128)(2,1)S(1)} %get-tuple-element.14), channel_id=1, source_target_pairs={{0,12},{1,13},{2,14},{3,15},{4,0},{5,1},{6,2},{7,3},{8,4},{9,5},{1... | collective-permute-start | bytes 393224 | tf_op jit(solution)/shard_map/ppermute | solution.py:38
  104.0 7.7 %collective-permute-start.19 = (bf16[128,1024]{1,0:T(8,128)(2,1)S(1)}, bf16[128,1024]{1,0:T(8,128)(2,1)S(1)}, u32[]{:S(2)}, u32[]{:S(2)}) collective-permute-start(bf16[128,1024]{1,0:T(8,128)(2,1)S(1)} %pad_maximum_fusion.2), channel_id=1, source_target_pairs={{0,12},{1,13},{2,14},{3,15},{4,0},{5,1},{6,2},{7,3},{8,4},{9,5},{1... | collective-permute-start | bytes 786440 | tf_op jit(solution)/shard_map/ppermute | solution.py:38
  107.0 8.2 %collective-permute-start.17 = (bf16[128,1024]{1,0:T(8,128)(2,1)S(1)}, bf16[128,1024]{1,0:T(8,128)(2,1)S(1)}, u32[]{:S(2)}, u32[]{:S(2)}) collective-permute-start(bf16[128,1024]{1,0:T(8,128)(2,1)S(1)} %pad_maximum_fusion.1), channel_id=1, source_target_pairs={{0,4},{1,5},{2,6},{3,7},{4,8},{5,9},{6,10},{7,11},{8,12},{9,13},{1... | collective-permute-start | bytes 786440 | tf_op jit(solution)/shard_map/ppermute | solution.py:38
  115.4 8.8 %collective-permute-start.22 = (bf16[32,1024]{1,0:T(8,128)(2,1)S(1)}, bf16[32,1024]{1,0:T(8,128)(2,1)S(1)}, u32[]{:S(2)}, u32[]{:S(2)}) collective-permute-start(bf16[32,1024]{1,0:T(8,128)(2,1)S(1)} %get-tuple-element.22), channel_id=1, source_target_pairs={{0,2},{1,3},{2,0},{3,1},{4,6},{5,7},{6,4},{7,5},{8,10},{9,11},{10,... | collective-permute-start | bytes 196616 | tf_op jit(solution)/shard_map/ppermute | solution.py:38
  117.6 7.9 %collective-permute-start.20 = (bf16[32,1024]{1,0:T(8,128)(2,1)S(1)}, bf16[32,1024]{1,0:T(8,128)(2,1)S(1)}, u32[]{:S(2)}, u32[]{:S(2)}) collective-permute-start(bf16[32,1024]{1,0:T(8,128)(2,1)S(1)} %get-tuple-element.21), channel_id=1, source_target_pairs={{0,16},{1,17},{2,18},{3,19},{4,20},{5,21},{6,22},{7,23},{8,24},{9,... | collective-permute-start | bytes 196616 | tf_op jit(solution)/shard_map/ppermute | solution.py:38
  123.5 7.6 %collective-permute-start.21 = (bf16[32,1024]{1,0:T(8,128)(2,1)S(1)}, bf16[32,1024]{1,0:T(8,128)(2,1)S(1)}, u32[]{:S(2)}, u32[]{:S(2)}) collective-permute-start(bf16[32,1024]{1,0:T(8,128)(2,1)S(1)} %get-tuple-element.23), channel_id=1, source_target_pairs={{0,18},{1,19},{2,16},{3,17},{4,22},{5,23},{6,20},{7,21},{8,26},{9,... | collective-permute-start | bytes 196616 | tf_op jit(solution)/shard_map/ppermute | solution.py:38

commit v2 on v1

v2 whole, which is shorter than its diff:
```python
import functools

import jax
import jax.numpy as jnp
from jax import lax
from jax.experimental import pallas as pl
from jax.experimental.pallas import tpu as pltpu
from jax.sharding import PartitionSpec as P

AXES = ("ao", "pair")
BLK = 64
TILES = 16
PAIRS = TILES // 2
NAO = 2048
RW = 1024
COLS = 128
PIECE = NAO // 8
META = 16
BODY = PAIRS * 128
PAY = BODY + META
GROUPS = 8
DEPTH = GROUPS * 512
BF = jnp.bfloat16
F32 = jnp.float32


def device_of(index):
    ao, pair = index // 16, index % 16
    return ao // 8, ao % 8, pair // 4, (pair // 2) % 2, pair % 2


def index_of(x_hi, z, y, x_lo, core):
    return ((x_hi % 2) * 8 + z % 8) * 16 + ((y % 4) * 2 + x_lo % 2) * 2 + core % 2


def permute(value, where):
    pairs = [(source, index_of(*where(*device_of(source)))) for source in range(256)]
    return lax.ppermute(value, AXES, pairs)


def along_y(value, steps):
    return permute(value, lambda x_hi, z, y, x_lo, core: (x_hi, z, y + steps, x_lo, core))


def along_z(value, steps):
    return permute(value, lambda x_hi, z, y, x_lo, core: (x_hi, z + steps, y, x_lo, core))


def swap_x(value):
    return permute(value, lambda x_hi, z, y, x_lo, core: (x_hi, z, y, x_lo + 1, core))


def swap_core(value):
    return permute(value, lambda x_hi, z, y, x_lo, core: (x_hi, z, y, x_lo, core + 1))


def next_group(value, flip):
    def where(x_hi, z, y, x_lo, core):
        return (x_hi + (z == 7), z + 1, y, x_lo + flip, core)

    return permute(value, where)


def scatter_target(x_hi, z, y, x_lo, core):
    target_y, target_x, target_core = x_hi * 2 + z // 4, (z // 2) % 2, z % 2
    target_hi = x_hi + (x_lo - target_x) % 2
    return target_hi, z + 3 - 2 * ((y - target_y) % 4) + core, target_y, target_x, target_core


def scatter_pieces(green_occ, green_virtual, x_hi, z, y, core):
    target_z = (z + 11 - 2 * ((y - x_hi * 2 - z // 4 + 4) % 4) + core) % 8
    both = jnp.concatenate([green_occ, green_virtual], axis=1)
    starts = (target_z * PIECE, (target_z + 4) % 8 * PIECE)
    return jnp.concatenate([lax.dynamic_slice_in_dim(both, start, PIECE, 0) for start in starts], axis=0)


def pack_kernel(orbital_ref, window_ref, count_ref, tile_ref, out_ref, order_ref):
    live = count_ref[0]
    windows = [window_ref[slot] for slot in range(TILES)]
    keys = [
        jnp.where(slot < live, windows[slot], TILES) * TILES + slot for slot in range(TILES)
    ]
    ranks = [jnp.int32(0) for slot in range(TILES)]
    for first in range(TILES):
        for second in range(first + 1, TILES):
            later = (keys[second] < keys[first]).astype(jnp.int32)
            ranks[first] = ranks[first] + later
            ranks[second] = ranks[second] + (1 - later)
    for slot in range(TILES):
        order_ref[ranks[slot]] = slot
    lane = lax.broadcasted_iota(jnp.int32, (META, 128), 1)
    meta = jnp.where(lane == 32, live, jnp.zeros((META, 128), jnp.int32))
    last = jnp.int32(0)
    for slot in range(TILES):
        source = order_ref[slot]
        last = jnp.where(slot < live, window_ref[source], last)
        meta = jnp.where(lane == slot, last, meta)
        meta = jnp.where(lane == TILES + slot, orbital_ref[source], meta)
    for index in range(PAIRS):
        rows = []
        for slot in (2 * index, 2 * index + 1):
            rows.append(jnp.where(slot < live, tile_ref[order_ref[slot]].astype(F32), 0.0))
        both = jnp.concatenate(rows, axis=0)
        out_ref[pl.ds(index * 128, 128), :] = both.T.astype(BF)
    out_ref[pl.ds(BODY, META), :] = meta.astype(F32).astype(BF)


def pack(tile_orbital, tile_window, tile_count, tile_values):
    smem = pl.BlockSpec(memory_space=pltpu.SMEM)
    return pl.pallas_call(
        pack_kernel,
        out_shape=jax.ShapeDtypeStruct((PAY, 128), BF),
        in_specs=[smem, smem, smem, pl.BlockSpec(memory_space=pltpu.VMEM)],
        out_specs=pl.BlockSpec(memory_space=pltpu.VMEM),
        scratch_shapes=[pltpu.SMEM((TILES,), jnp.int32)],
    )(tile_orbital, tile_window, tile_count, tile_values)


def chi_kernel(
    place_ref, meta_ref, own_ref, east_ref, west_ref, far_a_ref, far_b_ref,
    green_ref, other_ref, keep0_ref, keep1_ref, keep2_ref, keep3_ref, send_ref, occ_ref, vir_ref, acc_ref,
):
    keep_refs = (keep0_ref, keep1_ref, keep2_ref, keep3_ref)
    my_z, my_y, my_x, my_core = place_ref[0], place_ref[1], place_ref[2], place_ref[3]
    occ_ref[...] = jnp.zeros_like(occ_ref)
    vir_ref[...] = jnp.zeros_like(vir_ref)
    def rows_of(orbital):
        piece = lax.rem(orbital // 4 - my_z + 8, 8)
        start = pl.multiple_of(piece * PIECE + lax.rem(orbital, 4) * BLK, BLK)
        return jnp.concatenate(
            [green_ref[pl.ds(start, BLK), :], other_ref[pl.ds(start, BLK), :]], axis=1
        )

    def store(block, window, column):
        high, y, x = window // 8, lax.rem(window // 2, 4), lax.rem(window, 2)
        dy, dx = lax.rem(y - my_y + 4, 4), lax.rem(x - my_x + 2, 2)
        spot = ((dy * 2 + dx) * 2 + high) * 32
        vir_row = pl.multiple_of(window * BLK, BLK)
        for i in range(2):
            part = block[i * BLK:(i + 1) * BLK]
            occ = jnp.concatenate([part[:, 0:128], part[:, 256:384]], axis=1)
            vir = jnp.concatenate([part[:, 128:256], part[:, 384:512]], axis=1)
            vir_ref[pl.ds(vir_row, BLK), pl.ds(column + i * 256, 256)] = vir
            for core in range(2):
                row = pl.multiple_of(jnp.where(my_core == core, 0, 512) + spot, 32)
                occ_ref[pl.ds(row, 32), pl.ds(column + i * 256, 256)] = occ[core * 32:(core + 1) * 32]

    lane = lax.broadcasted_iota(jnp.int32, (128, 128), 1) // BLK

    def group(tiles_ref, base, number):
        live = meta_ref[number, 2 * TILES]
        column = number * 512

        def step(index, carry):
            slots = [4 * index + t for t in range(4)]
            windows = [meta_ref[number, slot] for slot in slots]
            before = jnp.where(index > 0, meta_ref[number, jnp.maximum(slots[0] - 1, 0)], -1)
            halves = [
                tiles_ref[pl.ds(pl.multiple_of(base + index * 256 + k * 128, 16), 128), :]
                for k in range(2)
            ]
            zero = jnp.zeros_like(halves[0])
            stacked = []
            for t in range(4):
                parts = []
                for k in range(2):
                    even = (2 * k <= t) & (windows[min(2 * k, t)] == windows[t])
                    odd = (2 * k + 1 <= t) & (windows[min(2 * k + 1, t)] == windows[t])
                    if 2 * k > t:
                        parts.append(zero)
                    else:
                        keep = jnp.where(lane == 0, even.astype(jnp.int32) if not isinstance(even, bool) else int(even), odd.astype(jnp.int32) if not isinstance(odd, bool) else int(odd))
                        parts.append(jnp.where(keep > 0, halves[k], zero))
                stacked.append(jnp.concatenate(parts, axis=1))
            stacked = jnp.concatenate(stacked, axis=0)
            rows = jnp.concatenate([rows_of(meta_ref[number, TILES + slot]) for slot in slots], axis=0)

            def finish(product):
                acc_ref[...] = product[384:]
                half = product.astype(BF)
                for t in range(4):
                    store(half[t * 128:(t + 1) * 128], windows[t], column)

            @pl.when(windows[0] != before)
            def _():
                finish(jnp.dot(stacked, rows, preferred_element_type=F32))

            @pl.when(windows[0] == before)
            def _():
                product = jnp.dot(stacked, rows, preferred_element_type=F32)
                carried = acc_ref[...]
                finish(jnp.concatenate(
                    [product[t * 128:(t + 1) * 128] + jnp.where(windows[t] == before, carried, 0.0) for t in range(4)],
                    axis=0,
                ))

            return carry

        lax.fori_loop(0, lax.div(live + 3, 4), step, 0)

    number = 0
    for tiles_ref in (own_ref, east_ref, west_ref, far_a_ref, far_b_ref):
        for base in range(0, tiles_ref.shape[0], PAY):
            group(tiles_ref, base, number)
            number += 1

    def chi(row, rows):
        return lax.dot_general(
            occ_ref[pl.ds(row, rows), :], vir_ref[...], (((1,), (1,)), ((), ())), preferred_element_type=F32
        )

    send_ref[...] = chi(512, 512).astype(BF)
    product = chi(0, 512)
    for quarter in range(4):
        keep_refs[quarter][...] = product[quarter * 128:(quarter + 1) * 128]


def chi_call(place, meta, tiles, green, other):
    smem = pl.BlockSpec(memory_space=pltpu.SMEM)
    vmem = pl.BlockSpec(memory_space=pltpu.VMEM)
    return pl.pallas_call(
        chi_kernel,
        out_shape=(jax.ShapeDtypeStruct((128, RW), F32),) * 4 + (jax.ShapeDtypeStruct((512, RW), BF),),
        in_specs=[smem, smem] + [vmem] * 7,
        out_specs=(vmem,) * 5,
        scratch_shapes=[
            pltpu.VMEM((RW, DEPTH), BF),
            pltpu.VMEM((RW, DEPTH), BF),
            pltpu.VMEM((128, 512), F32),
        ],
        compiler_params=pltpu.CompilerParams(vmem_limit_bytes=48 * 1024 * 1024),
        cost_estimate=pl.CostEstimate(flops=12 * 10**9, bytes_accessed=8 * 2**20, transcendentals=0),
    )(place, meta, *tiles, green, other)


def together(*values):
    return lax.optimization_barrier(values)


def gather(payload, pieces):
    payload, pieces = together(payload, pieces)
    first = permute(pieces, scatter_target)
    own = jnp.concatenate([payload, swap_x(payload)], axis=0)
    own, first = together(own, first)
    below, above = along_z(first, 1), along_z(first, -1)
    east, west = along_y(own, 1), along_y(own, -1)
    below, above, east, west = together(below, above, east, west)
    near = swap_core(jnp.concatenate([first, above, below], axis=0))
    two_below, two_above = along_z(below[:PIECE], 1), along_z(above[:PIECE], -1)
    far_a, far_b = along_y(east[:PAY], 1), along_y(west[PAY:], -1)
    two_below, two_above, near = together(two_below, two_above, near)
    rest = swap_core(jnp.concatenate([two_above, two_below], axis=0))
    green = by_offset(first, above, below, two_above, two_below)
    other = by_offset(
        near[:2 * PIECE], near[2 * PIECE:4 * PIECE], near[4 * PIECE:], rest[:PIECE], rest[PIECE:]
    )
    return (own, east, west, far_a, far_b), green, other


def by_offset(first, above, below, two_above, two_below):
    parts = (
        first[:PIECE], above[:PIECE], two_above, below[PIECE:],
        first[PIECE:], above[PIECE:], two_below, below[:PIECE],
    )
    return jnp.concatenate(parts, axis=0)


def reduce_band(keeps, send):
    got = swap_core(send)
    parts = [got[quarter * 128:(quarter + 1) * 128] for quarter in range(4)]
    across = keeps[2] + parts[2].astype(F32)
    ahead = along_y(across[:64].astype(BF), 1)
    behind = along_y(across[64:].astype(BF), -1)
    one, three = keeps[1] + parts[1].astype(F32), keeps[3] + parts[3].astype(F32)
    up = jnp.concatenate([one[:64] + ahead.astype(F32), one[64:]], axis=0).astype(BF)
    down = jnp.concatenate([three[:64], three[64:] + behind.astype(F32)], axis=0).astype(BF)
    up, down = along_y(up, 1), along_y(down, -1)
    total = keeps[0] + parts[0].astype(F32) + up.astype(F32) + down.astype(F32)
    upper = total[:32] + swap_x(total[64:96].astype(BF)).astype(F32)
    lower = next_group(total[32:64].astype(BF), 0).astype(F32) + next_group(total[96:].astype(BF), 1).astype(F32)
    return jnp.concatenate([lower[:, :512], lower[:, 512:] + upper[:, :512], upper[:, 512:]], axis=1)


def per_device(green_occ, green_virtual, tile_values, tile_orbital, tile_window, tile_count):
    ao, pair = lax.axis_index("ao"), lax.axis_index("pair")
    x_hi, z, y, x_lo, core = device_of(ao * 16 + pair)
    place = jnp.stack([z, y, x_lo, core]).astype(jnp.int32)
    pieces = scatter_pieces(green_occ, green_virtual, x_hi, z, y, core)
    payload = pack(tile_orbital, tile_window, tile_count, tile_values)
    tiles, green, other = gather(payload, pieces)
    rows = [part[start + BODY:start + BODY + 1, :64] for part in tiles for start in range(0, part.shape[0], PAY)]
    meta = jnp.concatenate(rows, axis=0).astype(jnp.int32)
    *keeps, send = chi_call(place, meta, tiles, green, other)
    return reduce_band(keeps, send)


def solution(mesh):
    in_specs = (
        P(None, "ao"),
        P(None, "ao"),
        P(("ao", "pair"), None, None),
        P(("ao", "pair")),
        P(("ao", "pair")),
        P(("ao", "pair")),
    )
    out_specs = P(("ao", "pair"), None)
    return jax.shard_map(
        per_device, mesh=mesh, in_specs=in_specs, out_specs=out_specs, check_vma=False
    )
```

time: 133 us -> 116 us (0.87)
  waiting for transfers between devices: 60.1 us -> 46.9 us
  local copies, waits for them, and re-layouts: 2.38 us -> 13.3 us
  starting transfers between devices: 39.8 us -> 31.3 us
  Pallas kernels: 24.8 us -> 19.4 us
    ppermute x23 -> x20, waiting for transfers between devices: 60.1 us -> 46.9 us  [permute(): return lax.ppermute(value, AXES, pairs)]
    unnamed x10 -> x17, local copies, waits for them, and re-layouts: 0.08 us -> 10.8 us
    ppermute x23 -> x20, starting transfers between devices: 39.8 us -> 31.3 us  [permute(): return lax.ppermute(value, AXES, pairs)]
    pallas_call x1, Pallas kernels: 22.7 us -> 17.3 us  [chi_call(): pl.pallas_call(chi_kernel, out_shape=(jax.ShapeDtypeStruct((128, RW), F32...]
    dynamic_slice x2 -> x1, local copies, waits for them, and re-layouts: 2.15 us -> 0.03 us  [scatter_pieces(): lax.dynamic_slice_in_dim(both, start, PIECE, 0)]
    concatenate x4 -> x6, other arithmetic: 0.09 us -> 2.01 us  [the longest x1 0.99 us: gather(): own = jnp.concatenate([payload, swap_x(payload)], axis=0)]
    concatenate x1 -> x3, local copies, waits for them, and re-layouts: 0.01 us -> 1.72 us  [the longest x2 1.59 us: by_offset(): return jnp.concatenate(parts, axis=0)]
    add x1, other arithmetic: 1.89 us -> 0.25 us  [reduce_band(): keeps[1] + parts[1].astype(F32)]
  transfers between devices with their start and end apart: 23 -> 20, of which waited for: 13 -> 12; matrix products, arithmetic and copies ran while one was open for 0% -> 7% of each run, Pallas kernels for 2% -> 0%
where the time goes in v2:
time: 116 us; the launch traced here: 115 us
  waiting for transfers between devices  46.9 us (40%)
  starting transfers between devices  31.3 us (27%)
  Pallas kernels  19.4 us (17%)
  local copies, waits for them, and re-layouts  13.3 us (11%)
  other arithmetic  3.32 us (3%)
    ppermute x20, waiting for transfers between devices, permute(): return lax.ppermute(value, AXES, pairs)  46.9 us
    ppermute x20, starting transfers between devices, permute(): return lax.ppermute(value, AXES, pairs)  31.3 us
    pallas_call x1, Pallas kernels, chi_call(): pl.pallas_call(chi_kernel, out_shape=(jax.ShapeDtypeStruct((128, RW), F32...  17.3 us
    unnamed x17, local copies, waits for them, and re-layouts  10.8 us
  transfers between devices with their start and end apart: 20, of which 12 were waited for; matrix products, arithmetic and copies ran while one was open for 7% of the time, Pallas kernels for 0%

profile of v2, /device:TPU:6, one launch (start us, length us, event | category | flops | bytes accessed | tf_op | source)
XLA Modules:
  0.0 115.1 jit_solution(13690219477402779411)
XLA Ops:
  0.0 1.2 %constant_dynamic-update-slice_fusion.1 = bf16[2048,256]{1,0:T(8,128)(2,1)S(1)} fusion(bf16[2048,128]{1,0:T(8,128)(2,1)} %param.6), kind=kLoop, calls=%fused_computation.33 | loop fusion | bytes 1048576
  1.9 0.1 constant_dynamic-update-slice_fusion
  2.1 2.1 %shard_map.64 = bf16[1040,128]{1,0:T(8,128)(2,1)} custom-call(s32[16]{0:T(128)} %orbital_ref.1, s32[16]{0:T(128)} %window_ref.1, s32[1]{0:T(128)S(6)} %copy.22.count_ref, bf16[16,64,128]{2,1,0:T(8,128)(2,1)} %tile_ref.1), custom_call_target="tpu_custom_call" | custom-call | tf_op jit(solution)/shard_map/pallas_call | solution.py:110
  4.1 0.8 collective-permute-start
  5.0 9.1 %collective-permute-start.1 = (bf16[512,256]{1,0:T(8,128)(2,1)S(1)}, bf16[512,256]{1,0:T(8,128)(2,1)S(1)}, u32[]{:S(2)}, u32[]{:S(2)}) collective-permute-start(bf16[512,256]{1,0:T(8,128)(2,1)S(1)} %pad_maximum_fusion.2), channel_id=1, source_target_pairs={{0,48},{1,64},{2,176},{3,192},{4,16},{5,32},{6,144},{7,160},{8,112... | collective-permute-start | bytes 786440 | tf_op jit(solution)/shard_map/ppermute | solution.py:38
  14.0 0.0 collective-permute-done
  14.0 1.0 pad_maximum_fusion.1.own_ref
  15.0 8.7 %collective-permute-done.1 = bf16[512,256]{1,0:T(8,128)(2,1)S(1)} collective-permute-done((bf16[512,256]{1,0:T(8,128)(2,1)S(1)}, bf16[512,256]{1,0:T(8,128)(2,1)S(1)}, u32[]{:S(2)}, u32[]{:S(2)}) %collective-permute-start.1) | collective-permute-done | bytes 262176 | tf_op jit(solution)/shard_map/ppermute | solution.py:38
  23.7 5.1 %collective-permute-start.4 = (bf16[2080,128]{1,0:T(8,128)(2,1)S(1)}, bf16[2080,128]{1,0:T(8,128)(2,1)S(1)}, u32[]{:S(2)}, u32[]{:S(2)}) collective-permute-start(bf16[2080,128]{1,0:T(8,128)(2,1)S(1)} %pad_maximum_fusion.1.own_ref), channel_id=1, source_target_pairs={{0,4},{1,5},{2,6},{3,7},{4,8},{5,9},{6,10},{7,11},{8,12},{9,13},{1... | collective-permute-start | bytes 1597448 | tf_op jit(solution)/shard_map/ppermute | solution.py:38
  28.8 0.0 collective-permute-start.5
  28.8 2.4 %collective-permute-start.2 = (bf16[512,256]{1,0:T(8,128)(2,1)S(1)}, bf16[512,256]{1,0:T(8,128)(2,1)S(1)}, u32[]{:S(2)}, u32[]{:S(2)}) collective-permute-start(bf16[512,256]{1,0:T(8,128)(2,1)S(1)} %collective-permute-done.1), channel_id=1, source_target_pairs={{0,16},{1,17},{2,18},{3,19},{4,20},{5,21},{6,22},{7,23},{8,24},{9,... | collective-permute-start | bytes 786440 | tf_op jit(solution)/shard_map/ppermute | solution.py:38
  31.2 0.8 collective-permute-start.3
  32.0 0.1 pad_add_fusion.place_ref
  32.1 5.9 %collective-permute-done.2 = bf16[512,256]{1,0:T(8,128)(2,1)S(1)} collective-permute-done((bf16[512,256]{1,0:T(8,128)(2,1)S(1)}, bf16[512,256]{1,0:T(8,128)(2,1)S(1)}, u32[]{:S(2)}, u32[]{:S(2)}) %collective-permute-start.2) | collective-permute-done | bytes 262176 | tf_op jit(solution)/shard_map/ppermute | solution.py:38
  38.0 0.0 collective-permute-done.3
  38.0 2.0 %collective-permute-done.4.east_ref = bf16[2080,128]{1,0:T(8,128)(2,1)S(1)} collective-permute-done((bf16[2080,128]{1,0:T(8,128)(2,1)S(1)}, bf16[2080,128]{1,0:T(8,128)(2,1)S(1)}, u32[]{:S(2)}, u32[]{:S(2)}) %collective-permute-start.4) | collective-permute-done | bytes 532512 | tf_op jit(solution)/shard_map/ppermute | solution.py:38
  39.9 2.2 %collective-permute-done.5.west_ref = bf16[2080,128]{1,0:T(8,128)(2,1)S(1)} collective-permute-done((bf16[2080,128]{1,0:T(8,128)(2,1)S(1)}, bf16[2080,128]{1,0:T(8,128)(2,1)S(1)}, u32[]{:S(2)}, u32[]{:S(2)}) %collective-permute-start.5) | collective-permute-done | bytes 532512 | tf_op jit(solution)/shard_map/ppermute | solution.py:38
  42.1 0.9 pad_maximum_fusion
  43.1 0.0 collective-permute-start.10
  43.1 0.7 slice_dynamic-update-slice_fusion.11
  43.7 0.4 collective-permute-start.6
  44.1 3.0 %collective-permute-start.7 = (bf16[1040,128]{1,0:T(8,128)(2,1)S(1)}, bf16[1040,128]{1,0:T(8,128)(2,1)S(1)}, u32[]{:S(2)}, u32[]{:S(2)}) collective-permute-start(bf16[1040,128]{1,0:T(8,128)(2,1)S(1)} %slice.152), channel_id=1, source_target_pairs={{0,12},{1,13},{2,14},{3,15},{4,0},{5,1},{6,2},{7,3},{8,4},{9,5},{1... | collective-permute-start | bytes 798728 | tf_op jit(solution)/shard_map/ppermute | solution.py:38
  47.2 0.7 fusion.8
  47.8 1.1 collective-permute-start.9
  48.9 1.0 collective-permute-start.8
  50.0 3.9 %collective-permute-done.6.far_a_ref = bf16[1040,128]{1,0:T(8,128)(2,1)S(1)} collective-permute-done((bf16[1040,128]{1,0:T(8,128)(2,1)S(1)}, bf16[1040,128]{1,0:T(8,128)(2,1)S(1)}, u32[]{:S(2)}, u32[]{:S(2)}) %collective-permute-start.6) | collective-permute-done | bytes 266272 | tf_op jit(solution)/shard_map/ppermute | solution.py:38
  53.8 0.0 collective-permute-done.7.far_b_ref
  53.9 0.0 collective-permute-done.9
  53.9 3.7 %collective-permute-done.8 = bf16[256,256]{1,0:T(8,128)(2,1)S(1)} collective-permute-done((bf16[256,256]{1,0:T(8,128)(2,1)S(1)}, bf16[256,256]{1,0:T(8,128)(2,1)S(1)}, u32[]{:S(2)}, u32[]{:S(2)}) %collective-permute-start.8) | collective-permute-done | bytes 131104 | tf_op jit(solution)/shard_map/ppermute | solution.py:38
  57.6 0.0 collective-permute-done.10
  57.6 0.1 collective-permute-start.11
  57.7 0.9 slice_dynamic-update-slice_fusion.7
  58.6 1.6 %slice_dynamic-update-slice_fusion.6 = (bf16[2048,256]{1,0:T(8,128)(2,1)S(1)}, bf16[2048,256]{1,0:T(8,128)(2,1)}) fusion(bf16[2048,256]{1,0:T(8,128)(2,1)S(1)} %slice_dynamic-update-slice_fusion.7, bf16[1536,256]{1,0:T(8,128)(2,1)} %collective-permute-done.10, bf16[2048,256]{1,0:T(8,128)(2,1)} %get-tuple-element.56, ...), kind=kLoop, calls=%fused_computation.25 | loop fusion | bytes 524288
  60.2 0.7 slice_dynamic-update-slice_fusion.10
  60.9 0.7 slice_dynamic-update-slice_fusion.9
  61.6 0.7 slice_dynamic-update-slice_fusion.8
  62.2 0.7 constant_dynamic-update-slice_fusion.3
  62.9 0.7 constant_dynamic-update-slice_fusion.2.green_ref
  63.6 0.0 collective-permute-done.11
  63.6 0.9 slice_dynamic-update-slice_fusion.5
  64.5 0.9 slice_dynamic-update-slice_fusion.4
  65.4 0.9 slice_dynamic-update-slice_fusion.3
  66.4 0.9 slice_dynamic-update-slice_fusion.2.other_ref
  67.3 1.0 copy-done.1
  68.3 17.3 %shard_map.65 = (f32[128,1024]{1,0:T(8,128)S(1)}, f32[128,1024]{1,0:T(8,128)S(1)}, f32[128,1024]{1,0:T(8,128)S(1)}, f32[128,1024]{1,0:T(8,128)S(1)}, bf16[512,1024]{1,0:T(8,128)(2,1)S(1)}) custom-call(s32[4]{0:T(128)S(1)} %pad_add_fusion.place_ref, s32[8,64]{1,0:T(8,128)S(1)} %convert_element_type.43.meta_ref, ...), custom_call_target="tpu_custom_call" | custom-call | flops 12000000000 | bytes 8388608 | tf_op jit(solution)/shard_map/pallas_call | solution.py:221
  85.6 0.2 collective-permute-start.12
  85.8 2.5 %collective-permute-done.12 = bf16[512,1024]{1,0:T(8,128)(2,1)S(1)} collective-permute-done((bf16[512,1024]{1,0:T(8,128)(2,1)S(1)}, bf16[512,1024]{1,0:T(8,128)(2,1)S(1)}, u32[]{:S(2)}, u32[]{:S(2)}) %collective-permute-start.12) | collective-permute-done | bytes 1048608 | tf_op jit(solution)/shard_map/ppermute | solution.py:38
  88.3 0.3 convert_add_fusion.2
  88.6 0.1 collective-permute-start.13
  88.7 3.5 %collective-permute-start.15 = (bf16[64,1024]{1,0:T(8,128)(2,1)S(1)}, bf16[64,1024]{1,0:T(8,128)(2,1)S(1)}, u32[]{:S(2)}, u32[]{:S(2)}) collective-permute-start(bf16[64,1024]{1,0:T(8,128)(2,1)S(1)} %get-tuple-element.54), channel_id=1, source_target_pairs={{0,12},{1,13},{2,14},{3,15},{4,0},{5,1},{6,2},{7,3},{8,4},{9,5},{1... | collective-permute-start | bytes 393224 | tf_op jit(solution)/shard_map/ppermute | solution.py:38
  92.3 3.2 %collective-permute-done.13 = bf16[64,1024]{1,0:T(8,128)(2,1)S(1)} collective-permute-done((bf16[64,1024]{1,0:T(8,128)(2,1)S(1)}, bf16[64,1024]{1,0:T(8,128)(2,1)S(1)}, u32[]{:S(2)}, u32[]{:S(2)}) %collective-permute-start.13) | collective-permute-done | bytes 131104 | tf_op jit(solution)/shard_map/ppermute | solution.py:38
  95.5 0.1 collective-permute-start.14
  95.6 0.0 collective-permute-done.15
  95.7 3.3 %collective-permute-start.16 = (bf16[128,1024]{1,0:T(8,128)(2,1)S(1)}, bf16[128,1024]{1,0:T(8,128)(2,1)S(1)}, u32[]{:S(2)}, u32[]{:S(2)}) collective-permute-start(bf16[128,1024]{1,0:T(8,128)(2,1)S(1)} %pad_maximum_fusion.5), channel_id=1, source_target_pairs={{0,12},{1,13},{2,14},{3,15},{4,0},{5,1},{6,2},{7,3},{8,4},{9,5},{1... | collective-permute-start | bytes 786440 | tf_op jit(solution)/shard_map/ppermute | solution.py:38
  99.0 5.3 %collective-permute-done.14 = bf16[128,1024]{1,0:T(8,128)(2,1)S(1)} collective-permute-done((bf16[128,1024]{1,0:T(8,128)(2,1)S(1)}, bf16[128,1024]{1,0:T(8,128)(2,1)S(1)}, u32[]{:S(2)}, u32[]{:S(2)}) %collective-permute-start.14) | collective-permute-done | bytes 262176 | tf_op jit(solution)/shard_map/ppermute | solution.py:38
  104.3 0.0 collective-permute-done.16
  104.3 0.2 fusion.2
  104.5 0.3 collective-permute-start.19
  104.8 0.0 collective-permute-start.17
  104.8 0.0 collective-permute-start.18
  104.8 4.8 %collective-permute-done.19 = bf16[32,1024]{1,0:T(8,128)(2,1)S(1)} collective-permute-done((bf16[32,1024]{1,0:T(8,128)(2,1)S(1)}, bf16[32,1024]{1,0:T(8,128)(2,1)S(1)}, u32[]{:S(2)}, u32[]{:S(2)}) %collective-permute-start.19) | collective-permute-done | bytes 65568 | tf_op jit(solution)/shard_map/ppermute | solution.py:38
  109.6 3.1 %collective-permute-done.17 = bf16[32,1024]{1,0:T(8,128)(2,1)S(1)} collective-permute-done((bf16[32,1024]{1,0:T(8,128)(2,1)S(1)}, bf16[32,1024]{1,0:T(8,128)(2,1)S(1)}, u32[]{:S(2)}, u32[]{:S(2)}) %collective-permute-start.17) | collective-permute-done | bytes 65568 | tf_op jit(solution)/shard_map/ppermute | solution.py:38
  112.6 1.7 %collective-permute-done.18 = bf16[32,1024]{1,0:T(8,128)(2,1)S(1)} collective-permute-done((bf16[32,1024]{1,0:T(8,128)(2,1)S(1)}, bf16[32,1024]{1,0:T(8,128)(2,1)S(1)}, u32[]{:S(2)}, u32[]{:S(2)}) %collective-permute-start.18) | collective-permute-done | bytes 65568 | tf_op jit(solution)/shard_map/ppermute | solution.py:38
  114.4 0.7 pad_maximum_fusion.6
  (28 shorter events, 0.4 us)
Async XLA Ops:
  0.0 1.9 %copy-start = (bf16[2048,128]{1,0:T(8,128)(2,1)S(1)}, bf16[2048,128]{1,0:T(8,128)(2,1)}, u32[]{:S(2)}) copy-start(bf16[2048,128]{1,0:T(8,128)(2,1)} %param.7) | copy-start | bytes 1572868
  4.1 9.9 %collective-permute-start = (bf16[1040,128]{1,0:T(8,128)(2,1)}, bf16[1040,128]{1,0:T(8,128)(2,1)S(1)}, u32[]{:S(2)}, u32[]{:S(2)}) collective-permute-start(bf16[1040,128]{1,0:T(8,128)(2,1)} %shard_map.64), channel_id=1, source_target_pairs={{0,2},{1,3},{2,0},{3,1},{4,6},{5,7},{6,4},{7,5},{8,10},{9,11},{10,... | collective-permute-start | bytes 798728 | tf_op jit(solution)/shard_map/ppermute | solution.py:38
  5.0 18.8 %collective-permute-start.1 = (bf16[512,256]{1,0:T(8,128)(2,1)S(1)}, bf16[512,256]{1,0:T(8,128)(2,1)S(1)}, u32[]{:S(2)}, u32[]{:S(2)}) collective-permute-start(bf16[512,256]{1,0:T(8,128)(2,1)S(1)} %pad_maximum_fusion.2), channel_id=1, source_target_pairs={{0,48},{1,64},{2,176},{3,192},{4,16},{5,32},{6,144},{7,160},{8,112... | collective-permute-start | bytes 786440 | tf_op jit(solution)/shard_map/ppermute | solution.py:38
  23.7 16.2 %collective-permute-start.4 = (bf16[2080,128]{1,0:T(8,128)(2,1)S(1)}, bf16[2080,128]{1,0:T(8,128)(2,1)S(1)}, u32[]{:S(2)}, u32[]{:S(2)}) collective-permute-start(bf16[2080,128]{1,0:T(8,128)(2,1)S(1)} %pad_maximum_fusion.1.own_ref), channel_id=1, source_target_pairs={{0,4},{1,5},{2,6},{3,7},{4,8},{5,9},{6,10},{7,11},{8,12},{9,13},{1... | collective-permute-start | bytes 1597448 | tf_op jit(solution)/shard_map/ppermute | solution.py:38
  28.8 13.3 %collective-permute-start.5 = (bf16[2080,128]{1,0:T(8,128)(2,1)S(1)}, bf16[2080,128]{1,0:T(8,128)(2,1)S(1)}, u32[]{:S(2)}, u32[]{:S(2)}) collective-permute-start(bf16[2080,128]{1,0:T(8,128)(2,1)S(1)} %pad_maximum_fusion.1.own_ref), channel_id=1, source_target_pairs={{0,12},{1,13},{2,14},{3,15},{4,0},{5,1},{6,2},{7,3},{8,4},{9,5},{1... | collective-permute-start | bytes 1597448 | tf_op jit(solution)/shard_map/ppermute | solution.py:38
  28.8 9.2 %collective-permute-start.2 = (bf16[512,256]{1,0:T(8,128)(2,1)S(1)}, bf16[512,256]{1,0:T(8,128)(2,1)S(1)}, u32[]{:S(2)}, u32[]{:S(2)}) collective-permute-start(bf16[512,256]{1,0:T(8,128)(2,1)S(1)} %collective-permute-done.1), channel_id=1, source_target_pairs={{0,16},{1,17},{2,18},{3,19},{4,20},{5,21},{6,22},{7,23},{8,24},{9,... | collective-permute-start | bytes 786440 | tf_op jit(solution)/shard_map/ppermute | solution.py:38
  31.2 6.7 %collective-permute-start.3 = (bf16[512,256]{1,0:T(8,128)(2,1)S(1)}, bf16[512,256]{1,0:T(8,128)(2,1)S(1)}, u32[]{:S(2)}, u32[]{:S(2)}) collective-permute-start(bf16[512,256]{1,0:T(8,128)(2,1)S(1)} %collective-permute-done.1), channel_id=1, source_target_pairs={{0,112},{1,113},{2,114},{3,115},{4,116},{5,117},{6,118},{7,119},{8... | collective-permute-start | bytes 786440 | tf_op jit(solution)/shard_map/ppermute | solution.py:38
  43.1 14.5 %collective-permute-start.10 = (bf16[1536,256]{1,0:T(8,128)(2,1)}, bf16[1536,256]{1,0:T(8,128)(2,1)}, u32[]{:S(2)}, u32[]{:S(2)}) collective-permute-start(bf16[1536,256]{1,0:T(8,128)(2,1)} %pad_maximum_fusion), channel_id=1, source_target_pairs={{0,1},{1,0},{2,3},{3,2},{4,5},{5,4},{6,7},{7,6},{8,9},{9,8},{10,11... | collective-permute-start | bytes 2359304 | tf_op jit(solution)/shard_map/ppermute | solution.py:38
  43.7 10.1 %collective-permute-start.6 = (bf16[1040,128]{1,0:T(8,128)(2,1)S(1)}, bf16[1040,128]{1,0:T(8,128)(2,1)S(1)}, u32[]{:S(2)}, u32[]{:S(2)}) collective-permute-start(bf16[1040,128]{1,0:T(8,128)(2,1)S(1)} %slice.150), channel_id=1, source_target_pairs={{0,4},{1,5},{2,6},{3,7},{4,8},{5,9},{6,10},{7,11},{8,12},{9,13},{1... | collective-permute-start | bytes 798728 | tf_op jit(solution)/shard_map/ppermute | solution.py:38
  44.1 9.7 %collective-permute-start.7 = (bf16[1040,128]{1,0:T(8,128)(2,1)S(1)}, bf16[1040,128]{1,0:T(8,128)(2,1)S(1)}, u32[]{:S(2)}, u32[]{:S(2)}) collective-permute-start(bf16[1040,128]{1,0:T(8,128)(2,1)S(1)} %slice.152), channel_id=1, source_target_pairs={{0,12},{1,13},{2,14},{3,15},{4,0},{5,1},{6,2},{7,3},{8,4},{9,5},{1... | collective-permute-start | bytes 798728 | tf_op jit(solution)/shard_map/ppermute | solution.py:38
  47.8 6.1 %collective-permute-start.9 = (bf16[256,256]{1,0:T(8,128)(2,1)S(1)}, bf16[256,256]{1,0:T(8,128)(2,1)S(1)}, u32[]{:S(2)}, u32[]{:S(2)}) collective-permute-start(bf16[256,256]{1,0:T(8,128)(2,1)S(1)} %get-tuple-element.55), channel_id=1, source_target_pairs={{0,112},{1,113},{2,114},{3,115},{4,116},{5,117},{6,118},{7,119},{8... | collective-permute-start | bytes 393224 | tf_op jit(solution)/shard_map/ppermute | solution.py:38
  48.9 8.7 %collective-permute-start.8 = (bf16[256,256]{1,0:T(8,128)(2,1)S(1)}, bf16[256,256]{1,0:T(8,128)(2,1)S(1)}, u32[]{:S(2)}, u32[]{:S(2)}) collective-permute-start(bf16[256,256]{1,0:T(8,128)(2,1)S(1)} %slice.156), channel_id=1, source_target_pairs={{0,16},{1,17},{2,18},{3,19},{4,20},{5,21},{6,22},{7,23},{8,24},{9,... | collective-permute-start | bytes 393224 | tf_op jit(solution)/shard_map/ppermute | solution.py:38
  57.6 6.0 %collective-permute-start.11 = (bf16[512,256]{1,0:T(8,128)(2,1)S(1)}, bf16[512,256]{1,0:T(8,128)(2,1)S(1)}, u32[]{:S(2)}, u32[]{:S(2)}) collective-permute-start(bf16[512,256]{1,0:T(8,128)(2,1)S(1)} %pad_maximum_fusion.3), channel_id=1, source_target_pairs={{0,1},{1,0},{2,3},{3,2},{4,5},{5,4},{6,7},{7,6},{8,9},{9,8},{10,11... | collective-permute-start | bytes 786440 | tf_op jit(solution)/shard_map/ppermute | solution.py:38
  67.3 1.0 copy-start.1
  85.6 2.7 %collective-permute-start.12 = (bf16[512,1024]{1,0:T(8,128)(2,1)S(1)}, bf16[512,1024]{1,0:T(8,128)(2,1)S(1)}, u32[]{:S(2)}, u32[]{:S(2)}) collective-permute-start(bf16[512,1024]{1,0:T(8,128)(2,1)S(1)} %get-tuple-element.33), channel_id=1, source_target_pairs={{0,1},{1,0},{2,3},{3,2},{4,5},{5,4},{6,7},{7,6},{8,9},{9,8},{10,11... | collective-permute-start | bytes 3145736 | tf_op jit(solution)/shard_map/ppermute | solution.py:38
  88.6 6.8 %collective-permute-start.13 = (bf16[64,1024]{1,0:T(8,128)(2,1)S(1)}, bf16[64,1024]{1,0:T(8,128)(2,1)S(1)}, u32[]{:S(2)}, u32[]{:S(2)}) collective-permute-start(bf16[64,1024]{1,0:T(8,128)(2,1)S(1)} %get-tuple-element.53), channel_id=1, source_target_pairs={{0,4},{1,5},{2,6},{3,7},{4,8},{5,9},{6,10},{7,11},{8,12},{9,13},{1... | collective-permute-start | bytes 393224 | tf_op jit(solution)/shard_map/ppermute | solution.py:38
  88.7 6.9 %collective-permute-start.15 = (bf16[64,1024]{1,0:T(8,128)(2,1)S(1)}, bf16[64,1024]{1,0:T(8,128)(2,1)S(1)}, u32[]{:S(2)}, u32[]{:S(2)}) collective-permute-start(bf16[64,1024]{1,0:T(8,128)(2,1)S(1)} %get-tuple-element.54), channel_id=1, source_target_pairs={{0,12},{1,13},{2,14},{3,15},{4,0},{5,1},{6,2},{7,3},{8,4},{9,5},{1... | collective-permute-start | bytes 393224 | tf_op jit(solution)/shard_map/ppermute | solution.py:38
  95.5 8.8 %collective-permute-start.14 = (bf16[128,1024]{1,0:T(8,128)(2,1)S(1)}, bf16[128,1024]{1,0:T(8,128)(2,1)S(1)}, u32[]{:S(2)}, u32[]{:S(2)}) collective-permute-start(bf16[128,1024]{1,0:T(8,128)(2,1)S(1)} %pad_maximum_fusion.4), channel_id=1, source_target_pairs={{0,4},{1,5},{2,6},{3,7},{4,8},{5,9},{6,10},{7,11},{8,12},{9,13},{1... | collective-permute-start | bytes 786440 | tf_op jit(solution)/shard_map/ppermute | solution.py:38
  95.7 8.6 %collective-permute-start.16 = (bf16[128,1024]{1,0:T(8,128)(2,1)S(1)}, bf16[128,1024]{1,0:T(8,128)(2,1)S(1)}, u32[]{:S(2)}, u32[]{:S(2)}) collective-permute-start(bf16[128,1024]{1,0:T(8,128)(2,1)S(1)} %pad_maximum_fusion.5), channel_id=1, source_target_pairs={{0,12},{1,13},{2,14},{3,15},{4,0},{5,1},{6,2},{7,3},{8,4},{9,5},{1... | collective-permute-start | bytes 786440 | tf_op jit(solution)/shard_map/ppermute | solution.py:38
  104.5 5.1 %collective-permute-start.19 = (bf16[32,1024]{1,0:T(8,128)(2,1)S(1)}, bf16[32,1024]{1,0:T(8,128)(2,1)S(1)}, u32[]{:S(2)}, u32[]{:S(2)}) collective-permute-start(bf16[32,1024]{1,0:T(8,128)(2,1)S(1)} %get-tuple-element.51), channel_id=1, source_target_pairs={{0,2},{1,3},{2,0},{3,1},{4,6},{5,7},{6,4},{7,5},{8,10},{9,11},{10,... | collective-permute-start | bytes 196616 | tf_op jit(solution)/shard_map/ppermute | solution.py:38
  104.8 7.9 %collective-permute-start.17 = (bf16[32,1024]{1,0:T(8,128)(2,1)S(1)}, bf16[32,1024]{1,0:T(8,128)(2,1)S(1)}, u32[]{:S(2)}, u32[]{:S(2)}) collective-permute-start(bf16[32,1024]{1,0:T(8,128)(2,1)S(1)} %get-tuple-element.50), channel_id=1, source_target_pairs={{0,16},{1,17},{2,18},{3,19},{4,20},{5,21},{6,22},{7,23},{8,24},{9,... | collective-permute-start | bytes 196616 | tf_op jit(solution)/shard_map/ppermute | solution.py:38
  104.8 9.6 %collective-permute-start.18 = (bf16[32,1024]{1,0:T(8,128)(2,1)S(1)}, bf16[32,1024]{1,0:T(8,128)(2,1)S(1)}, u32[]{:S(2)}, u32[]{:S(2)}) collective-permute-start(bf16[32,1024]{1,0:T(8,128)(2,1)S(1)} %get-tuple-element.52), channel_id=1, source_target_pairs={{0,18},{1,19},{2,16},{3,17},{4,22},{5,23},{6,20},{7,21},{8,26},{9,... | collective-permute-start | bytes 196616 | tf_op jit(solution)/shard_map/ppermute | solution.py:38

commit v3 on v2

--- a/solution.py
+++ b/solution.py
@@ -61,14 +61,18 @@
     return permute(value, where)
 
 
+Z_OFFSETS = (3, 6, 1, 5, 7, 0, 4, 2)
+
+
 def scatter_target(x_hi, z, y, x_lo, core):
-    target_y, target_x, target_core = x_hi * 2 + z // 4, (z // 2) % 2, z % 2
+    target_y, target_x, target_core = z % 4, x_hi, z // 4
     target_hi = x_hi + (x_lo - target_x) % 2
-    return target_hi, z + 3 - 2 * ((y - target_y) % 4) + core, target_y, target_x, target_core
-
-
-def scatter_pieces(green_occ, green_virtual, x_hi, z, y, core):
-    target_z = (z + 11 - 2 * ((y - x_hi * 2 - z // 4 + 4) % 4) + core) % 8
+    return target_hi, z + Z_OFFSETS[(y - target_y) % 4 * 2 + core], target_y, target_x, target_core
+
+
+def scatter_pieces(green_occ, green_virtual, z, y, core):
+    case = (y - z % 4 + 4) % 4 * 2 + core
+    target_z = (z + sum(offset * (case == number) for number, offset in enumerate(Z_OFFSETS))) % 8
     both = jnp.concatenate([green_occ, green_virtual], axis=1)
     starts = (target_z * PIECE, (target_z + 4) % 8 * PIECE)
     return jnp.concatenate([lax.dynamic_slice_in_dim(both, start, PIECE, 0) for start in starts], axis=0)
@@ -118,18 +122,29 @@
 
 def chi_kernel(
     place_ref, meta_ref, own_ref, east_ref, west_ref, far_a_ref, far_b_ref,
-    green_ref, other_ref, keep0_ref, keep1_ref, keep2_ref, keep3_ref, send_ref, occ_ref, vir_ref, acc_ref,
+    first_ref, above_ref, below_ref, two_above_ref, two_below_ref, near_ref, rest_ref,
+    keep0_ref, keep1_ref, keep2_ref, keep3_ref, send_ref, green_ref, occ_ref, vir_ref,
 ):
     keep_refs = (keep0_ref, keep1_ref, keep2_ref, keep3_ref)
     my_z, my_y, my_x, my_core = place_ref[0], place_ref[1], place_ref[2], place_ref[3]
     occ_ref[...] = jnp.zeros_like(occ_ref)
     vir_ref[...] = jnp.zeros_like(vir_ref)
+
+    own_parts = (
+        (first_ref, 0, 0), (first_ref, 1, 4), (above_ref, 0, 1), (above_ref, 1, 5),
+        (below_ref, 0, 7), (below_ref, 1, 3), (two_above_ref, 0, 2), (two_below_ref, 0, 6),
+    )
+    other_parts = (
+        (near_ref, 0, 0), (near_ref, 1, 4), (near_ref, 2, 1), (near_ref, 3, 5),
+        (near_ref, 4, 7), (near_ref, 5, 3), (rest_ref, 0, 2), (rest_ref, 1, 6),
+    )
+    for lanes, parts in ((0, own_parts), (256, other_parts)):
+        for ref, spot, offset in parts:
+            start = pl.multiple_of(lax.rem(my_z + offset, 8) * PIECE, PIECE)
+            green_ref[pl.ds(start, PIECE), lanes:lanes + 256] = ref[spot * PIECE:(spot + 1) * PIECE, :]
+
     def rows_of(orbital):
-        piece = lax.rem(orbital // 4 - my_z + 8, 8)
-        start = pl.multiple_of(piece * PIECE + lax.rem(orbital, 4) * BLK, BLK)
-        return jnp.concatenate(
-            [green_ref[pl.ds(start, BLK), :], other_ref[pl.ds(start, BLK), :]], axis=1
-        )
+        return green_ref[pl.ds(pl.multiple_of(orbital * BLK, BLK), BLK), :]
 
     def store(block, window, column):
         high, y, x = window // 8, lax.rem(window // 2, 4), lax.rem(window, 2)
@@ -145,58 +160,44 @@
                 row = pl.multiple_of(jnp.where(my_core == core, 0, 512) + spot, 32)
                 occ_ref[pl.ds(row, 32), pl.ds(column + i * 256, 256)] = occ[core * 32:(core + 1) * 32]
 
-    lane = lax.broadcasted_iota(jnp.int32, (128, 128), 1) // BLK
+    lane = lax.broadcasted_iota(jnp.int32, (1, 128), 1)
+    low = jnp.where(lane < BLK, 1.0, 0.0).astype(BF)
+    high = jnp.where(lane < BLK, 0.0, 1.0).astype(BF)
+    blank = jnp.zeros((128, 128), BF)
+
+    def slots_of(tiles_ref, base, number, quads):
+        column = number * 512
+        total = None
+        for quad in range(quads):
+            pair = [tiles_ref[base + quad * 256 + k * 128:base + quad * 256 + (k + 1) * 128, :] for k in range(2)]
+            stacked = jnp.concatenate([
+                jnp.concatenate([pair[0] * low, blank], axis=1),
+                jnp.concatenate([pair[0] * high, blank], axis=1),
+                jnp.concatenate([blank, pair[1] * low], axis=1),
+                jnp.concatenate([blank, pair[1] * high], axis=1),
+            ], axis=0)
+            slots = [4 * quad + t for t in range(4)]
+            rows = jnp.concatenate([rows_of(meta_ref[number, TILES + slot]) for slot in slots], axis=0)
+            product = jnp.dot(stacked, rows, preferred_element_type=F32)
+            for t, slot in enumerate(slots):
+                window = meta_ref[number, slot]
+                fresh = product[t * 128:(t + 1) * 128]
+                if total is None:
+                    total = fresh
+                else:
+                    total = fresh + jnp.where(window == meta_ref[number, slot - 1], total, 0.0)
+                store(total.astype(BF), window, column)
 
     def group(tiles_ref, base, number):
         live = meta_ref[number, 2 * TILES]
-        column = number * 512
-
-        def step(index, carry):
-            slots = [4 * index + t for t in range(4)]
-            windows = [meta_ref[number, slot] for slot in slots]
-            before = jnp.where(index > 0, meta_ref[number, jnp.maximum(slots[0] - 1, 0)], -1)
-            halves = [
-                tiles_ref[pl.ds(pl.multiple_of(base + index * 256 + k * 128, 16), 128), :]
-                for k in range(2)
-            ]
-            zero = jnp.zeros_like(halves[0])
-            stacked = []
-            for t in range(4):
-                parts = []
-                for k in range(2):
-                    even = (2 * k <= t) & (windows[min(2 * k, t)] == windows[t])
-                    odd = (2 * k + 1 <= t) & (windows[min(2 * k + 1, t)] == windows[t])
-                    if 2 * k > t:
-                        parts.append(zero)
-                    else:
-                        keep = jnp.where(lane == 0, even.astype(jnp.int32) if not isinstance(even, bool) else int(even), odd.astype(jnp.int32) if not isinstance(odd, bool) else int(odd))
-                        parts.append(jnp.where(keep > 0, halves[k], zero))
-                stacked.append(jnp.concatenate(parts, axis=1))
-            stacked = jnp.concatenate(stacked, axis=0)
-            rows = jnp.concatenate([rows_of(meta_ref[number, TILES + slot]) for slot in slots], axis=0)
-
-            def finish(product):
-                acc_ref[...] = product[384:]
-                half = product.astype(BF)
-                for t in range(4):
-                    store(half[t * 128:(t + 1) * 128], windows[t], column)
-
-            @pl.when(windows[0] != before)
-            def _():
-                finish(jnp.dot(stacked, rows, preferred_element_type=F32))
-
-            @pl.when(windows[0] == before)
-            def _():
-                product = jnp.dot(stacked, rows, preferred_element_type=F32)
-                carried = acc_ref[...]
-                finish(jnp.concatenate(
-                    [product[t * 128:(t + 1) * 128] + jnp.where(windows[t] == before, carried, 0.0) for t in range(4)],
-                    axis=0,
-                ))
-
-            return carry
-
-        lax.fori_loop(0, lax.div(live + 3, 4), step, 0)
+
+        @pl.when(live <= 8)
+        def _():
+            slots_of(tiles_ref, base, number, 2)
+
+        @pl.when(live > 8)
+        def _():
+            slots_of(tiles_ref, base, number, 4)
 
     number = 0
     for tiles_ref in (own_ref, east_ref, west_ref, far_a_ref, far_b_ref):
@@ -215,22 +216,22 @@
         keep_refs[quarter][...] = product[quarter * 128:(quarter + 1) * 128]
 
 
-def chi_call(place, meta, tiles, green, other):
+def chi_call(place, meta, tiles, parts):
     smem = pl.BlockSpec(memory_space=pltpu.SMEM)
     vmem = pl.BlockSpec(memory_space=pltpu.VMEM)
     return pl.pallas_call(
         chi_kernel,
         out_shape=(jax.ShapeDtypeStruct((128, RW), F32),) * 4 + (jax.ShapeDtypeStruct((512, RW), BF),),
-        in_specs=[smem, smem] + [vmem] * 7,
+        in_specs=[smem, smem] + [vmem] * 12,
         out_specs=(vmem,) * 5,
         scratch_shapes=[
+            pltpu.VMEM((NAO, 512), BF),
             pltpu.VMEM((RW, DEPTH), BF),
             pltpu.VMEM((RW, DEPTH), BF),
-            pltpu.VMEM((128, 512), F32),
         ],
-        compiler_params=pltpu.CompilerParams(vmem_limit_bytes=48 * 1024 * 1024),
+        compiler_params=pltpu.CompilerParams(vmem_limit_bytes=32 * 1024 * 1024),
         cost_estimate=pl.CostEstimate(flops=12 * 10**9, bytes_accessed=8 * 2**20, transcendentals=0),
-    )(place, meta, *tiles, green, other)
+    )(place, meta, *tiles, *parts)
 
 
 def together(*values):
@@ -238,7 +239,6 @@
 
 
 def gather(payload, pieces):
-    payload, pieces = together(payload, pieces)
     first = permute(pieces, scatter_target)
     own = jnp.concatenate([payload, swap_x(payload)], axis=0)
     own, first = together(own, first)
@@ -250,19 +250,7 @@
     far_a, far_b = along_y(east[:PAY], 1), along_y(west[PAY:], -1)
     two_below, two_above, near = together(two_below, two_above, near)
     rest = swap_core(jnp.concatenate([two_above, two_below], axis=0))
-    green = by_offset(first, above, below, two_above, two_below)
-    other = by_offset(
-        near[:2 * PIECE], near[2 * PIECE:4 * PIECE], near[4 * PIECE:], rest[:PIECE], rest[PIECE:]
-    )
-    return (own, east, west, far_a, far_b), green, other
-
-
-def by_offset(first, above, below, two_above, two_below):
-    parts = (
-        first[:PIECE], above[:PIECE], two_above, below[PIECE:],
-        first[PIECE:], above[PIECE:], two_below, below[:PIECE],
-    )
-    return jnp.concatenate(parts, axis=0)
+    return (own, east, west, far_a, far_b), (first, above, below, two_above, two_below, near, rest)
 
 
 def reduce_band(keeps, send):
@@ -285,12 +273,12 @@
     ao, pair = lax.axis_index("ao"), lax.axis_index("pair")
     x_hi, z, y, x_lo, core = device_of(ao * 16 + pair)
     place = jnp.stack([z, y, x_lo, core]).astype(jnp.int32)
-    pieces = scatter_pieces(green_occ, green_virtual, x_hi, z, y, core)
+    pieces = scatter_pieces(green_occ, green_virtual, z, y, core)
     payload = pack(tile_orbital, tile_window, tile_count, tile_values)
-    tiles, green, other = gather(payload, pieces)
+    tiles, parts = gather(payload, pieces)
     rows = [part[start + BODY:start + BODY + 1, :64] for part in tiles for start in range(0, part.shape[0], PAY)]
     meta = jnp.concatenate(rows, axis=0).astype(jnp.int32)
-    *keeps, send = chi_call(place, meta, tiles, green, other)
+    *keeps, send = chi_call(place, meta, tiles, parts)
     return reduce_band(keeps, send)
 
 

time: 116 us -> 104 us (0.90)
  local copies, waits for them, and re-layouts: 13.3 us -> 6.09 us
  waiting for transfers between devices: 46.9 us -> 43.7 us
  Pallas kernels: 19.4 us -> 17.8 us
    unnamed x17 -> x13, local copies, waits for them, and re-layouts: 10.8 us -> 4.46 us
    ppermute x20, waiting for transfers between devices: 46.9 us -> 43.7 us  [permute(): return lax.ppermute(value, AXES, pairs)]
    concatenate x2 -> x0, local copies, waits for them, and re-layouts: 1.59 us -> none  [by_offset(): return jnp.concatenate(parts, axis=0)]
    pallas_call x1, Pallas kernels: 17.3 us -> 15.7 us  [chi_call(): pl.pallas_call(chi_kernel, out_shape=(jax.ShapeDtypeStruct((128, RW), F32...]
  transfers between devices with their start and end apart: 20 -> 20, of which waited for: 12 -> 15; matrix products, arithmetic and copies ran while one was open for 7% -> 4% of each run, Pallas kernels for 0% -> 0%
where the time goes in v3:
time: 104 us
  waiting for transfers between devices  43.7 us (42%)
  starting transfers between devices  31.7 us (30%)
  Pallas kernels  17.8 us (17%)
  local copies, waits for them, and re-layouts  6.09 us (6%)
  other arithmetic  3.05 us (3%)
  between operations  1.11 us (1%)
    ppermute x20, waiting for transfers between devices, permute(): return lax.ppermute(value, AXES, pairs)  43.7 us
    ppermute x20, starting transfers between devices, permute(): return lax.ppermute(value, AXES, pairs)  31.7 us
    pallas_call x1, Pallas kernels, chi_call(): pl.pallas_call(chi_kernel, out_shape=(jax.ShapeDtypeStruct((128, RW), F32...  15.7 us
    unnamed x13, local copies, waits for them, and re-layouts  4.46 us
  transfers between devices with their start and end apart: 20, of which 15 were waited for; matrix products, arithmetic and copies ran while one was open for 4% of the time, Pallas kernels for 0%

profile of v3, /device:TPU:6, one launch (start us, length us, event | category | flops | bytes accessed | tf_op | source)
XLA Modules:
  0.0 103.5 jit_solution(1820196736712604843)
XLA Ops:
  0.0 0.0 copy-start.5
  0.7 2.1 %shard_map.64 = bf16[1040,128]{1,0:T(8,128)(2,1)} custom-call(s32[16]{0:T(128)} %orbital_ref.1, s32[16]{0:T(128)} %window_ref.1, s32[1]{0:T(128)S(6)} %copy.8.count_ref, bf16[16,64,128]{2,1,0:T(8,128)(2,1)} %tile_ref.1), custom_call_target="tpu_custom_call" | custom-call | tf_op jit(solution)/shard_map/pallas_call | solution.py:114
  2.8 0.8 collective-permute-start
  3.6 1.1 %constant_dynamic-update-slice_fusion.1 = bf16[2048,256]{1,0:T(8,128)(2,1)S(1)} fusion(bf16[2048,128]{1,0:T(8,128)(2,1)} %param.6), kind=kLoop, calls=%fused_computation.21 | loop fusion | bytes 1048576
  4.7 0.0 copy-done.5
  4.7 0.0 copy-start.4
  4.8 0.1 constant_dynamic-update-slice_fusion
  5.1 4.7 %collective-permute-start.1 = (bf16[512,256]{1,0:T(8,128)(2,1)S(1)}, bf16[512,256]{1,0:T(8,128)(2,1)S(1)}, u32[]{:S(2)}, u32[]{:S(2)}) collective-permute-start(bf16[512,256]{1,0:T(8,128)(2,1)S(1)} %pad_maximum_fusion.2), channel_id=1, source_target_pairs={{0,48},{1,96},{2,176},{3,224},{4,16},{5,80},{6,144},{7,208},{8,112... | collective-permute-start | bytes 786440 | tf_op jit(solution)/shard_map/ppermute | solution.py:38
  9.8 1.3 %collective-permute-done = bf16[1040,128]{1,0:T(8,128)(2,1)S(1)} collective-permute-done((bf16[1040,128]{1,0:T(8,128)(2,1)}, bf16[1040,128]{1,0:T(8,128)(2,1)S(1)}, u32[]{:S(2)}, u32[]{:S(2)}) %collective-permute-start) | collective-permute-done | bytes 266272 | tf_op jit(solution)/shard_map/ppermute | solution.py:38
  11.1 0.0 copy-done.4
  11.2 2.6 %collective-permute-done.1.first_ref = bf16[512,256]{1,0:T(8,128)(2,1)S(1)} collective-permute-done((bf16[512,256]{1,0:T(8,128)(2,1)S(1)}, bf16[512,256]{1,0:T(8,128)(2,1)S(1)}, u32[]{:S(2)}, u32[]{:S(2)}) %collective-permute-start.1) | collective-permute-done | bytes 262176 | tf_op jit(solution)/shard_map/ppermute | solution.py:38
  13.8 9.9 %collective-permute-start.5 = (bf16[2080,128]{1,0:T(8,128)(2,1)S(1)}, bf16[2080,128]{1,0:T(8,128)(2,1)S(1)}, u32[]{:S(2)}, u32[]{:S(2)}) collective-permute-start(bf16[2080,128]{1,0:T(8,128)(2,1)S(1)} %pad_maximum_fusion.1.own_ref), channel_id=1, source_target_pairs={{0,12},{1,13},{2,14},{3,15},{4,0},{5,1},{6,2},{7,3},{8,4},{9,5},{1... | collective-permute-start | bytes 1597448 | tf_op jit(solution)/shard_map/ppermute | solution.py:38
  23.7 0.0 collective-permute-start.4
  23.7 5.1 %collective-permute-start.3 = (bf16[512,256]{1,0:T(8,128)(2,1)S(1)}, bf16[512,256]{1,0:T(8,128)(2,1)S(1)}, u32[]{:S(2)}, u32[]{:S(2)}) collective-permute-start(bf16[512,256]{1,0:T(8,128)(2,1)S(1)} %collective-permute-done.1.first_ref), channel_id=1, source_target_pairs={{0,112},{1,113},{2,114},{3,115},{4,116},{5,117},{6,118},{7,119},{8... | collective-permute-start | bytes 786440 | tf_op jit(solution)/shard_map/ppermute | solution.py:38
  28.8 0.0 collective-permute-start.2
  28.8 3.9 %collective-permute-done.3.above_ref = bf16[512,256]{1,0:T(8,128)(2,1)S(1)} collective-permute-done((bf16[512,256]{1,0:T(8,128)(2,1)S(1)}, bf16[512,256]{1,0:T(8,128)(2,1)S(1)}, u32[]{:S(2)}, u32[]{:S(2)}) %collective-permute-start.3) | collective-permute-done | bytes 262176 | tf_op jit(solution)/shard_map/ppermute | solution.py:38
  32.7 3.7 %collective-permute-done.2.below_ref = bf16[512,256]{1,0:T(8,128)(2,1)S(1)} collective-permute-done((bf16[512,256]{1,0:T(8,128)(2,1)S(1)}, bf16[512,256]{1,0:T(8,128)(2,1)S(1)}, u32[]{:S(2)}, u32[]{:S(2)}) %collective-permute-start.2) | collective-permute-done | bytes 262176 | tf_op jit(solution)/shard_map/ppermute | solution.py:38
  36.4 0.0 collective-permute-done.5.west_ref
  36.4 3.2 %collective-permute-done.4.east_ref = bf16[2080,128]{1,0:T(8,128)(2,1)S(1)} collective-permute-done((bf16[2080,128]{1,0:T(8,128)(2,1)S(1)}, bf16[2080,128]{1,0:T(8,128)(2,1)S(1)}, u32[]{:S(2)}, u32[]{:S(2)}) %collective-permute-start.4) | collective-permute-done | bytes 532512 | tf_op jit(solution)/shard_map/ppermute | solution.py:38
  39.6 1.0 pad_maximum_fusion
  40.5 0.0 collective-permute-start.10
  40.5 0.7 slice.108
  41.2 0.7 slice.107
  41.9 0.0 collective-permute-start.8
  41.9 3.2 %collective-permute-start.9 = (bf16[256,256]{1,0:T(8,128)(2,1)}, bf16[256,256]{1,0:T(8,128)(2,1)S(1)}, u32[]{:S(2)}, u32[]{:S(2)}) collective-permute-start(bf16[256,256]{1,0:T(8,128)(2,1)} %slice.108), channel_id=1, source_target_pairs={{0,112},{1,113},{2,114},{3,115},{4,116},{5,117},{6,118},{7,119},{8... | collective-permute-start | bytes 393224 | tf_op jit(solution)/shard_map/ppermute | solution.py:38
  45.1 0.1 pad_add_fusion.place_ref
  45.2 0.5 collective-permute-start.7
  45.7 1.6 %collective-permute-start.6 = (bf16[1040,128]{1,0:T(8,128)(2,1)S(1)}, bf16[1040,128]{1,0:T(8,128)(2,1)S(1)}, u32[]{:S(2)}, u32[]{:S(2)}) collective-permute-start(bf16[1040,128]{1,0:T(8,128)(2,1)S(1)} %slice.103), channel_id=1, source_target_pairs={{0,4},{1,5},{2,6},{3,7},{4,8},{5,9},{6,10},{7,11},{8,12},{9,13},{1... | collective-permute-start | bytes 798728 | tf_op jit(solution)/shard_map/ppermute | solution.py:38
  47.3 1.9 %collective-permute-done.8.two_below_ref = bf16[256,256]{1,0:T(8,128)(2,1)S(1)} collective-permute-done((bf16[256,256]{1,0:T(8,128)(2,1)}, bf16[256,256]{1,0:T(8,128)(2,1)S(1)}, u32[]{:S(2)}, u32[]{:S(2)}) %collective-permute-start.8) | collective-permute-done | bytes 131104 | tf_op jit(solution)/shard_map/ppermute | solution.py:38
  49.2 0.0 collective-permute-done.9.two_above_ref
  49.2 0.0 collective-permute-done.10.near_ref
  49.2 0.7 pad_maximum_fusion.3
  49.9 0.0 collective-permute-start.11
  49.9 3.6 %collective-permute-done.7.far_b_ref = bf16[1040,128]{1,0:T(8,128)(2,1)S(1)} collective-permute-done((bf16[1040,128]{1,0:T(8,128)(2,1)S(1)}, bf16[1040,128]{1,0:T(8,128)(2,1)S(1)}, u32[]{:S(2)}, u32[]{:S(2)}) %collective-permute-start.7) | collective-permute-done | bytes 266272 | tf_op jit(solution)/shard_map/ppermute | solution.py:38
  53.5 0.0 copy-start
  53.5 0.7 copy-done
  54.3 0.6 collective-permute-done.6.far_a_ref
  54.8 0.0 copy-start.2
  54.8 0.7 copy-done.2
  55.6 0.0 collective-permute-done.11.rest_ref
  55.6 0.0 copy-start.1
  55.6 0.9 copy-done.1
  56.6 0.0 copy-start.3
  56.6 0.9 copy-done.3
  57.5 15.7 %shard_map.65 = (f32[128,1024]{1,0:T(8,128)S(1)}, f32[128,1024]{1,0:T(8,128)S(1)}, f32[128,1024]{1,0:T(8,128)S(1)}, f32[128,1024]{1,0:T(8,128)S(1)}, bf16[512,1024]{1,0:T(8,128)(2,1)S(1)}) custom-call(s32[4]{0:T(128)S(1)} %pad_add_fusion.place_ref, s32[8,64]{1,0:T(8,128)S(1)} %convert_element_type.53.meta_ref, ...), custom_call_target="tpu_custom_call" | custom-call | flops 12000000000 | bytes 8388608 | tf_op jit(solution)/shard_map/pallas_call | solution.py:222
  73.3 0.1 collective-permute-start.12
  73.4 2.6 %collective-permute-done.12 = bf16[512,1024]{1,0:T(8,128)(2,1)S(1)} collective-permute-done((bf16[512,1024]{1,0:T(8,128)(2,1)S(1)}, bf16[512,1024]{1,0:T(8,128)(2,1)S(1)}, u32[]{:S(2)}, u32[]{:S(2)}) %collective-permute-start.12) | collective-permute-done | bytes 1048608 | tf_op jit(solution)/shard_map/ppermute | solution.py:38
  76.0 0.2 convert_add_fusion.2
  76.3 1.0 collective-permute-start.15
  77.3 1.2 %collective-permute-start.13 = (bf16[64,1024]{1,0:T(8,128)(2,1)S(1)}, bf16[64,1024]{1,0:T(8,128)(2,1)S(1)}, u32[]{:S(2)}, u32[]{:S(2)}) collective-permute-start(bf16[64,1024]{1,0:T(8,128)(2,1)S(1)} %get-tuple-element.49), channel_id=1, source_target_pairs={{0,4},{1,5},{2,6},{3,7},{4,8},{5,9},{6,10},{7,11},{8,12},{9,13},{1... | collective-permute-start | bytes 393224 | tf_op jit(solution)/shard_map/ppermute | solution.py:38
  78.5 3.4 %collective-permute-done.15 = bf16[64,1024]{1,0:T(8,128)(2,1)S(1)} collective-permute-done((bf16[64,1024]{1,0:T(8,128)(2,1)S(1)}, bf16[64,1024]{1,0:T(8,128)(2,1)S(1)}, u32[]{:S(2)}, u32[]{:S(2)}) %collective-permute-start.15) | collective-permute-done | bytes 131104 | tf_op jit(solution)/shard_map/ppermute | solution.py:38
  82.0 2.2 %collective-permute-start.16 = (bf16[128,1024]{1,0:T(8,128)(2,1)S(1)}, bf16[128,1024]{1,0:T(8,128)(2,1)S(1)}, u32[]{:S(2)}, u32[]{:S(2)}) collective-permute-start(bf16[128,1024]{1,0:T(8,128)(2,1)S(1)} %pad_maximum_fusion.5), channel_id=1, source_target_pairs={{0,12},{1,13},{2,14},{3,15},{4,0},{5,1},{6,2},{7,3},{8,4},{9,5},{1... | collective-permute-start | bytes 786440 | tf_op jit(solution)/shard_map/ppermute | solution.py:38
  84.1 0.0 collective-permute-done.13
  84.2 0.1 collective-permute-start.14
  84.3 5.2 %collective-permute-done.16 = bf16[128,1024]{1,0:T(8,128)(2,1)S(1)} collective-permute-done((bf16[128,1024]{1,0:T(8,128)(2,1)S(1)}, bf16[128,1024]{1,0:T(8,128)(2,1)S(1)}, u32[]{:S(2)}, u32[]{:S(2)}) %collective-permute-start.16) | collective-permute-done | bytes 262176 | tf_op jit(solution)/shard_map/ppermute | solution.py:38
  89.6 3.2 %collective-permute-done.14 = bf16[128,1024]{1,0:T(8,128)(2,1)S(1)} collective-permute-done((bf16[128,1024]{1,0:T(8,128)(2,1)S(1)}, bf16[128,1024]{1,0:T(8,128)(2,1)S(1)}, u32[]{:S(2)}, u32[]{:S(2)}) %collective-permute-start.14) | collective-permute-done | bytes 262176 | tf_op jit(solution)/shard_map/ppermute | solution.py:38
  92.7 0.2 fusion.2
  92.9 0.1 collective-permute-start.19
  93.0 0.1 collective-permute-start.17
  93.1 1.1 %collective-permute-start.18 = (bf16[32,1024]{1,0:T(8,128)(2,1)S(1)}, bf16[32,1024]{1,0:T(8,128)(2,1)S(1)}, u32[]{:S(2)}, u32[]{:S(2)}) collective-permute-start(bf16[32,1024]{1,0:T(8,128)(2,1)S(1)} %get-tuple-element.48), channel_id=1, source_target_pairs={{0,18},{1,19},{2,16},{3,17},{4,22},{5,23},{6,20},{7,21},{8,26},{9,... | collective-permute-start | bytes 196616 | tf_op jit(solution)/shard_map/ppermute | solution.py:38
  94.2 3.8 %collective-permute-done.19 = bf16[32,1024]{1,0:T(8,128)(2,1)S(1)} collective-permute-done((bf16[32,1024]{1,0:T(8,128)(2,1)S(1)}, bf16[32,1024]{1,0:T(8,128)(2,1)S(1)}, u32[]{:S(2)}, u32[]{:S(2)}) %collective-permute-start.19) | collective-permute-done | bytes 65568 | tf_op jit(solution)/shard_map/ppermute | solution.py:38
  98.0 3.0 %collective-permute-done.17 = bf16[32,1024]{1,0:T(8,128)(2,1)S(1)} collective-permute-done((bf16[32,1024]{1,0:T(8,128)(2,1)S(1)}, bf16[32,1024]{1,0:T(8,128)(2,1)S(1)}, u32[]{:S(2)}, u32[]{:S(2)}) %collective-permute-start.17) | collective-permute-done | bytes 65568 | tf_op jit(solution)/shard_map/ppermute | solution.py:38
  101.0 1.8 %collective-permute-done.18 = bf16[32,1024]{1,0:T(8,128)(2,1)S(1)} collective-permute-done((bf16[32,1024]{1,0:T(8,128)(2,1)S(1)}, bf16[32,1024]{1,0:T(8,128)(2,1)S(1)}, u32[]{:S(2)}, u32[]{:S(2)}) %collective-permute-start.18) | collective-permute-done | bytes 65568 | tf_op jit(solution)/shard_map/ppermute | solution.py:38
  102.8 0.7 pad_maximum_fusion.6
  (22 shorter events, 0.4 us)
Async XLA Ops:
  0.0 4.7 %copy-start.5 = (bf16[2048,128]{1,0:T(8,128)(2,1)S(1)}, bf16[2048,128]{1,0:T(8,128)(2,1)}, u32[]{:S(2)}) copy-start(bf16[2048,128]{1,0:T(8,128)(2,1)} %param.7) | copy-start | bytes 1572868
  2.8 8.3 %collective-permute-start = (bf16[1040,128]{1,0:T(8,128)(2,1)}, bf16[1040,128]{1,0:T(8,128)(2,1)S(1)}, u32[]{:S(2)}, u32[]{:S(2)}) collective-permute-start(bf16[1040,128]{1,0:T(8,128)(2,1)} %shard_map.64), channel_id=1, source_target_pairs={{0,2},{1,3},{2,0},{3,1},{4,6},{5,7},{6,4},{7,5},{8,10},{9,11},{10,... | collective-permute-start | bytes 798728 | tf_op jit(solution)/shard_map/ppermute | solution.py:38
  4.7 6.4 %copy-start.4 = (bf16[1040,128]{1,0:T(8,128)(2,1)S(1)}, bf16[1040,128]{1,0:T(8,128)(2,1)}, u32[]{:S(2)}) copy-start(bf16[1040,128]{1,0:T(8,128)(2,1)} %shard_map.64) | copy-start | bytes 798724
  5.1 8.6 %collective-permute-start.1 = (bf16[512,256]{1,0:T(8,128)(2,1)S(1)}, bf16[512,256]{1,0:T(8,128)(2,1)S(1)}, u32[]{:S(2)}, u32[]{:S(2)}) collective-permute-start(bf16[512,256]{1,0:T(8,128)(2,1)S(1)} %pad_maximum_fusion.2), channel_id=1, source_target_pairs={{0,48},{1,96},{2,176},{3,224},{4,16},{5,80},{6,144},{7,208},{8,112... | collective-permute-start | bytes 786440 | tf_op jit(solution)/shard_map/ppermute | solution.py:38
  13.8 22.6 %collective-permute-start.5 = (bf16[2080,128]{1,0:T(8,128)(2,1)S(1)}, bf16[2080,128]{1,0:T(8,128)(2,1)S(1)}, u32[]{:S(2)}, u32[]{:S(2)}) collective-permute-start(bf16[2080,128]{1,0:T(8,128)(2,1)S(1)} %pad_maximum_fusion.1.own_ref), channel_id=1, source_target_pairs={{0,12},{1,13},{2,14},{3,15},{4,0},{5,1},{6,2},{7,3},{8,4},{9,5},{1... | collective-permute-start | bytes 1597448 | tf_op jit(solution)/shard_map/ppermute | solution.py:38
  23.7 15.9 %collective-permute-start.4 = (bf16[2080,128]{1,0:T(8,128)(2,1)S(1)}, bf16[2080,128]{1,0:T(8,128)(2,1)S(1)}, u32[]{:S(2)}, u32[]{:S(2)}) collective-permute-start(bf16[2080,128]{1,0:T(8,128)(2,1)S(1)} %pad_maximum_fusion.1.own_ref), channel_id=1, source_target_pairs={{0,4},{1,5},{2,6},{3,7},{4,8},{5,9},{6,10},{7,11},{8,12},{9,13},{1... | collective-permute-start | bytes 1597448 | tf_op jit(solution)/shard_map/ppermute | solution.py:38
  23.7 9.0 %collective-permute-start.3 = (bf16[512,256]{1,0:T(8,128)(2,1)S(1)}, bf16[512,256]{1,0:T(8,128)(2,1)S(1)}, u32[]{:S(2)}, u32[]{:S(2)}) collective-permute-start(bf16[512,256]{1,0:T(8,128)(2,1)S(1)} %collective-permute-done.1.first_ref), channel_id=1, source_target_pairs={{0,112},{1,113},{2,114},{3,115},{4,116},{5,117},{6,118},{7,119},{8... | collective-permute-start | bytes 786440 | tf_op jit(solution)/shard_map/ppermute | solution.py:38
  28.8 7.6 %collective-permute-start.2 = (bf16[512,256]{1,0:T(8,128)(2,1)S(1)}, bf16[512,256]{1,0:T(8,128)(2,1)S(1)}, u32[]{:S(2)}, u32[]{:S(2)}) collective-permute-start(bf16[512,256]{1,0:T(8,128)(2,1)S(1)} %collective-permute-done.1.first_ref), channel_id=1, source_target_pairs={{0,16},{1,17},{2,18},{3,19},{4,20},{5,21},{6,22},{7,23},{8,24},{9,... | collective-permute-start | bytes 786440 | tf_op jit(solution)/shard_map/ppermute | solution.py:38
  40.5 8.7 %collective-permute-start.10 = (bf16[1536,256]{1,0:T(8,128)(2,1)}, bf16[1536,256]{1,0:T(8,128)(2,1)S(1)}, u32[]{:S(2)}, u32[]{:S(2)}) collective-permute-start(bf16[1536,256]{1,0:T(8,128)(2,1)} %pad_maximum_fusion), channel_id=1, source_target_pairs={{0,1},{1,0},{2,3},{3,2},{4,5},{5,4},{6,7},{7,6},{8,9},{9,8},{10,11... | collective-permute-start | bytes 2359304 | tf_op jit(solution)/shard_map/ppermute | solution.py:38
  41.9 7.3 %collective-permute-start.8 = (bf16[256,256]{1,0:T(8,128)(2,1)}, bf16[256,256]{1,0:T(8,128)(2,1)S(1)}, u32[]{:S(2)}, u32[]{:S(2)}) collective-permute-start(bf16[256,256]{1,0:T(8,128)(2,1)} %slice.107), channel_id=1, source_target_pairs={{0,16},{1,17},{2,18},{3,19},{4,20},{5,21},{6,22},{7,23},{8,24},{9,... | collective-permute-start | bytes 393224 | tf_op jit(solution)/shard_map/ppermute | solution.py:38
  41.9 7.3 %collective-permute-start.9 = (bf16[256,256]{1,0:T(8,128)(2,1)}, bf16[256,256]{1,0:T(8,128)(2,1)S(1)}, u32[]{:S(2)}, u32[]{:S(2)}) collective-permute-start(bf16[256,256]{1,0:T(8,128)(2,1)} %slice.108), channel_id=1, source_target_pairs={{0,112},{1,113},{2,114},{3,115},{4,116},{5,117},{6,118},{7,119},{8... | collective-permute-start | bytes 393224 | tf_op jit(solution)/shard_map/ppermute | solution.py:38
  45.2 8.3 %collective-permute-start.7 = (bf16[1040,128]{1,0:T(8,128)(2,1)S(1)}, bf16[1040,128]{1,0:T(8,128)(2,1)S(1)}, u32[]{:S(2)}, u32[]{:S(2)}) collective-permute-start(bf16[1040,128]{1,0:T(8,128)(2,1)S(1)} %slice.105), channel_id=1, source_target_pairs={{0,12},{1,13},{2,14},{3,15},{4,0},{5,1},{6,2},{7,3},{8,4},{9,5},{1... | collective-permute-start | bytes 798728 | tf_op jit(solution)/shard_map/ppermute | solution.py:38
  45.7 9.1 %collective-permute-start.6 = (bf16[1040,128]{1,0:T(8,128)(2,1)S(1)}, bf16[1040,128]{1,0:T(8,128)(2,1)S(1)}, u32[]{:S(2)}, u32[]{:S(2)}) collective-permute-start(bf16[1040,128]{1,0:T(8,128)(2,1)S(1)} %slice.103), channel_id=1, source_target_pairs={{0,4},{1,5},{2,6},{3,7},{4,8},{5,9},{6,10},{7,11},{8,12},{9,13},{1... | collective-permute-start | bytes 798728 | tf_op jit(solution)/shard_map/ppermute | solution.py:38
  49.9 5.7 %collective-permute-start.11 = (bf16[512,256]{1,0:T(8,128)(2,1)}, bf16[512,256]{1,0:T(8,128)(2,1)}, u32[]{:S(2)}, u32[]{:S(2)}) collective-permute-start(bf16[512,256]{1,0:T(8,128)(2,1)} %pad_maximum_fusion.3), channel_id=1, source_target_pairs={{0,1},{1,0},{2,3},{3,2},{4,5},{5,4},{6,7},{7,6},{8,9},{9,8},{10,11... | collective-permute-start | bytes 786440 | tf_op jit(solution)/shard_map/ppermute | solution.py:38
  53.5 0.7 copy-start
  54.8 0.7 copy-start.2
  55.6 1.0 copy-start.1
  56.6 1.0 copy-start.3
  73.3 2.7 %collective-permute-start.12 = (bf16[512,1024]{1,0:T(8,128)(2,1)S(1)}, bf16[512,1024]{1,0:T(8,128)(2,1)S(1)}, u32[]{:S(2)}, u32[]{:S(2)}) collective-permute-start(bf16[512,1024]{1,0:T(8,128)(2,1)S(1)} %get-tuple-element.29), channel_id=1, source_target_pairs={{0,1},{1,0},{2,3},{3,2},{4,5},{5,4},{6,7},{7,6},{8,9},{9,8},{10,11... | collective-permute-start | bytes 3145736 | tf_op jit(solution)/shard_map/ppermute | solution.py:38
  76.3 5.6 %collective-permute-start.15 = (bf16[64,1024]{1,0:T(8,128)(2,1)S(1)}, bf16[64,1024]{1,0:T(8,128)(2,1)S(1)}, u32[]{:S(2)}, u32[]{:S(2)}) collective-permute-start(bf16[64,1024]{1,0:T(8,128)(2,1)S(1)} %get-tuple-element.50), channel_id=1, source_target_pairs={{0,12},{1,13},{2,14},{3,15},{4,0},{5,1},{6,2},{7,3},{8,4},{9,5},{1... | collective-permute-start | bytes 393224 | tf_op jit(solution)/shard_map/ppermute | solution.py:38
  77.3 6.9 %collective-permute-start.13 = (bf16[64,1024]{1,0:T(8,128)(2,1)S(1)}, bf16[64,1024]{1,0:T(8,128)(2,1)S(1)}, u32[]{:S(2)}, u32[]{:S(2)}) collective-permute-start(bf16[64,1024]{1,0:T(8,128)(2,1)S(1)} %get-tuple-element.49), channel_id=1, source_target_pairs={{0,4},{1,5},{2,6},{3,7},{4,8},{5,9},{6,10},{7,11},{8,12},{9,13},{1... | collective-permute-start | bytes 393224 | tf_op jit(solution)/shard_map/ppermute | solution.py:38
  82.0 7.6 %collective-permute-start.16 = (bf16[128,1024]{1,0:T(8,128)(2,1)S(1)}, bf16[128,1024]{1,0:T(8,128)(2,1)S(1)}, u32[]{:S(2)}, u32[]{:S(2)}) collective-permute-start(bf16[128,1024]{1,0:T(8,128)(2,1)S(1)} %pad_maximum_fusion.5), channel_id=1, source_target_pairs={{0,12},{1,13},{2,14},{3,15},{4,0},{5,1},{6,2},{7,3},{8,4},{9,5},{1... | collective-permute-start | bytes 786440 | tf_op jit(solution)/shard_map/ppermute | solution.py:38
  84.2 8.5 %collective-permute-start.14 = (bf16[128,1024]{1,0:T(8,128)(2,1)S(1)}, bf16[128,1024]{1,0:T(8,128)(2,1)S(1)}, u32[]{:S(2)}, u32[]{:S(2)}) collective-permute-start(bf16[128,1024]{1,0:T(8,128)(2,1)S(1)} %pad_maximum_fusion.4), channel_id=1, source_target_pairs={{0,4},{1,5},{2,6},{3,7},{4,8},{5,9},{6,10},{7,11},{8,12},{9,13},{1... | collective-permute-start | bytes 786440 | tf_op jit(solution)/shard_map/ppermute | solution.py:38
  92.9 5.1 %collective-permute-start.19 = (bf16[32,1024]{1,0:T(8,128)(2,1)S(1)}, bf16[32,1024]{1,0:T(8,128)(2,1)S(1)}, u32[]{:S(2)}, u32[]{:S(2)}) collective-permute-start(bf16[32,1024]{1,0:T(8,128)(2,1)S(1)} %get-tuple-element.47), channel_id=1, source_target_pairs={{0,2},{1,3},{2,0},{3,1},{4,6},{5,7},{6,4},{7,5},{8,10},{9,11},{10,... | collective-permute-start | bytes 196616 | tf_op jit(solution)/shard_map/ppermute | solution.py:38
  93.0 8.0 %collective-permute-start.17 = (bf16[32,1024]{1,0:T(8,128)(2,1)S(1)}, bf16[32,1024]{1,0:T(8,128)(2,1)S(1)}, u32[]{:S(2)}, u32[]{:S(2)}) collective-permute-start(bf16[32,1024]{1,0:T(8,128)(2,1)S(1)} %get-tuple-element.46), channel_id=1, source_target_pairs={{0,16},{1,17},{2,18},{3,19},{4,20},{5,21},{6,22},{7,23},{8,24},{9,... | collective-permute-start | bytes 196616 | tf_op jit(solution)/shard_map/ppermute | solution.py:38
  93.1 9.6 %collective-permute-start.18 = (bf16[32,1024]{1,0:T(8,128)(2,1)S(1)}, bf16[32,1024]{1,0:T(8,128)(2,1)S(1)}, u32[]{:S(2)}, u32[]{:S(2)}) collective-permute-start(bf16[32,1024]{1,0:T(8,128)(2,1)S(1)} %get-tuple-element.48), channel_id=1, source_target_pairs={{0,18},{1,19},{2,16},{3,17},{4,22},{5,23},{6,20},{7,21},{8,26},{9,... | collective-permute-start | bytes 196616 | tf_op jit(solution)/shard_map/ppermute | solution.py:38

commit v4 on v3

--- a/solution.py
+++ b/solution.py
@@ -70,12 +70,36 @@
     return target_hi, z + Z_OFFSETS[(y - target_y) % 4 * 2 + core], target_y, target_x, target_core
 
 
-def scatter_pieces(green_occ, green_virtual, z, y, core):
-    case = (y - z % 4 + 4) % 4 * 2 + core
-    target_z = (z + sum(offset * (case == number) for number, offset in enumerate(Z_OFFSETS))) % 8
-    both = jnp.concatenate([green_occ, green_virtual], axis=1)
-    starts = (target_z * PIECE, (target_z + 4) % 8 * PIECE)
-    return jnp.concatenate([lax.dynamic_slice_in_dim(both, start, PIECE, 0) for start in starts], axis=0)
+def cut_kernel(occ_ref, vir_ref, out_ref, sems):
+    ao, pair = lax.axis_index("ao"), lax.axis_index("pair")
+    z, y, core = lax.rem(ao, 8), pair // 4, lax.rem(pair, 2)
+    case = lax.rem(y - lax.rem(z, 4) + 4, 4) * 2 + core
+    target_z = z
+    for number, offset in enumerate(Z_OFFSETS):
+        target_z = target_z + jnp.where(case == number, offset, 0)
+    copies = []
+    for spot in range(2):
+        start = pl.multiple_of(lax.rem(target_z + 4 * spot, 8) * PIECE, PIECE)
+        for part, ref in enumerate((occ_ref, vir_ref)):
+            copies.append(pltpu.make_async_copy(
+                ref.at[pl.ds(start, PIECE)],
+                out_ref.at[pl.ds(spot * PIECE, PIECE), pl.ds(part * COLS, COLS)],
+                sems.at[spot * 2 + part],
+            ))
+    for copy in copies:
+        copy.start()
+    for copy in copies:
+        copy.wait()
+
+
+def cut_pieces(green_occ, green_virtual):
+    return pl.pallas_call(
+        cut_kernel,
+        out_shape=jax.ShapeDtypeStruct((2 * PIECE, 2 * COLS), BF),
+        in_specs=[pl.BlockSpec(memory_space=pl.ANY)] * 2,
+        out_specs=pl.BlockSpec(memory_space=pltpu.VMEM),
+        scratch_shapes=[pltpu.SemaphoreType.DMA((4,))],
+    )(green_occ, green_virtual)
 
 
 def pack_kernel(orbital_ref, window_ref, count_ref, tile_ref, out_ref, order_ref):
@@ -120,28 +144,34 @@
     )(tile_orbital, tile_window, tile_count, tile_values)
 
 
-def chi_kernel(
-    place_ref, meta_ref, own_ref, east_ref, west_ref, far_a_ref, far_b_ref,
-    first_ref, above_ref, below_ref, two_above_ref, two_below_ref, near_ref, rest_ref,
-    keep0_ref, keep1_ref, keep2_ref, keep3_ref, send_ref, green_ref, occ_ref, vir_ref,
-):
-    keep_refs = (keep0_ref, keep1_ref, keep2_ref, keep3_ref)
+def chi_kernel(place_ref, meta_ref, *refs):
+    tile_parts, green_parts = refs[:5], refs[5:15]
+    keep_refs, send_ref = refs[15:19], refs[19]
+    tiles_ref, green_ref, occ_ref, vir_ref, sems = refs[20:]
     my_z, my_y, my_x, my_core = place_ref[0], place_ref[1], place_ref[2], place_ref[3]
+
+    spots = []
+    for lanes in (0, 256):
+        spots += [(lanes, (0, 4)), (lanes, (1, 5)), (lanes, (7, 3)), (lanes, (2,)), (lanes, (6,))]
+    copies = []
+    for ref, (lanes, offsets) in zip(green_parts, spots):
+        for spot, offset in enumerate(offsets):
+            start = pl.multiple_of(lax.rem(my_z + offset, 8) * PIECE, PIECE)
+            copies.append((
+                ref.at[pl.ds(spot * PIECE, PIECE)], green_ref.at[pl.ds(start, PIECE), pl.ds(lanes, 256)]
+            ))
+    row = 0
+    for ref in tile_parts:
+        rows = ref.shape[0]
+        copies.append((ref, tiles_ref.at[pl.ds(row, rows)]))
+        row += rows
+    copies = [pltpu.make_async_copy(source, target, sems.at[k]) for k, (source, target) in enumerate(copies)]
+    for copy in copies:
+        copy.start()
     occ_ref[...] = jnp.zeros_like(occ_ref)
     vir_ref[...] = jnp.zeros_like(vir_ref)
-
-    own_parts = (
-        (first_ref, 0, 0), (first_ref, 1, 4), (above_ref, 0, 1), (above_ref, 1, 5),
-        (below_ref, 0, 7), (below_ref, 1, 3), (two_above_ref, 0, 2), (two_below_ref, 0, 6),
-    )
-    other_parts = (
-        (near_ref, 0, 0), (near_ref, 1, 4), (near_ref, 2, 1), (near_ref, 3, 5),
-        (near_ref, 4, 7), (near_ref, 5, 3), (rest_ref, 0, 2), (rest_ref, 1, 6),
-    )
-    for lanes, parts in ((0, own_parts), (256, other_parts)):
-        for ref, spot, offset in parts:
-            start = pl.multiple_of(lax.rem(my_z + offset, 8) * PIECE, PIECE)
-            green_ref[pl.ds(start, PIECE), lanes:lanes + 256] = ref[spot * PIECE:(spot + 1) * PIECE, :]
+    for copy in copies:
+        copy.wait()
 
     def rows_of(orbital):
         return green_ref[pl.ds(pl.multiple_of(orbital * BLK, BLK), BLK), :]
@@ -165,7 +195,7 @@
     high = jnp.where(lane < BLK, 0.0, 1.0).astype(BF)
     blank = jnp.zeros((128, 128), BF)
 
-    def slots_of(tiles_ref, base, number, quads):
+    def slots_of(base, number, quads):
         column = number * 512
         total = None
         for quad in range(quads):
@@ -188,22 +218,19 @@
                     total = fresh + jnp.where(window == meta_ref[number, slot - 1], total, 0.0)
                 store(total.astype(BF), window, column)
 
-    def group(tiles_ref, base, number):
+    def group(base, number):
         live = meta_ref[number, 2 * TILES]
 
         @pl.when(live <= 8)
         def _():
-            slots_of(tiles_ref, base, number, 2)
+            slots_of(base, number, 2)
 
         @pl.when(live > 8)
         def _():
-            slots_of(tiles_ref, base, number, 4)
-
-    number = 0
-    for tiles_ref in (own_ref, east_ref, west_ref, far_a_ref, far_b_ref):
-        for base in range(0, tiles_ref.shape[0], PAY):
-            group(tiles_ref, base, number)
-            number += 1
+            slots_of(base, number, 4)
+
+    for number in range(GROUPS):
+        group(number * PAY, number)
 
     def chi(row, rows):
         return lax.dot_general(
@@ -222,12 +249,14 @@
     return pl.pallas_call(
         chi_kernel,
         out_shape=(jax.ShapeDtypeStruct((128, RW), F32),) * 4 + (jax.ShapeDtypeStruct((512, RW), BF),),
-        in_specs=[smem, smem] + [vmem] * 12,
+        in_specs=[smem, smem] + [pl.BlockSpec(memory_space=pl.ANY)] * 15,
         out_specs=(vmem,) * 5,
         scratch_shapes=[
+            pltpu.VMEM((GROUPS * PAY, 128), BF),
             pltpu.VMEM((NAO, 512), BF),
             pltpu.VMEM((RW, DEPTH), BF),
             pltpu.VMEM((RW, DEPTH), BF),
+            pltpu.SemaphoreType.DMA((21,)),
         ],
         compiler_params=pltpu.CompilerParams(vmem_limit_bytes=32 * 1024 * 1024),
         cost_estimate=pl.CostEstimate(flops=12 * 10**9, bytes_accessed=8 * 2**20, transcendentals=0),
@@ -242,15 +271,15 @@
     first = permute(pieces, scatter_target)
     own = jnp.concatenate([payload, swap_x(payload)], axis=0)
     own, first = together(own, first)
-    below, above = along_z(first, 1), along_z(first, -1)
+    single = first[:PIECE]
+    green = [
+        first, along_z(first, -1), along_z(first, 1), along_z(single, -2), along_z(single, 2)
+    ]
     east, west = along_y(own, 1), along_y(own, -1)
-    below, above, east, west = together(below, above, east, west)
-    near = swap_core(jnp.concatenate([first, above, below], axis=0))
-    two_below, two_above = along_z(below[:PIECE], 1), along_z(above[:PIECE], -1)
+    *green, east, west = together(*green, east, west)
     far_a, far_b = along_y(east[:PAY], 1), along_y(west[PAY:], -1)
-    two_below, two_above, near = together(two_below, two_above, near)
-    rest = swap_core(jnp.concatenate([two_above, two_below], axis=0))
-    return (own, east, west, far_a, far_b), (first, above, below, two_above, two_below, near, rest)
+    green = green + [swap_core(part) for part in green]
+    return (own, east, west, far_a, far_b), green
 
 
 def reduce_band(keeps, send):
@@ -273,7 +302,8 @@
     ao, pair = lax.axis_index("ao"), lax.axis_index("pair")
     x_hi, z, y, x_lo, core = device_of(ao * 16 + pair)
     place = jnp.stack([z, y, x_lo, core]).astype(jnp.int32)
-    pieces = scatter_pieces(green_occ, green_virtual, z, y, core)
+    pieces = cut_pieces(green_occ, green_virtual)
+    tile_values, pieces = together(tile_values, pieces)
     payload = pack(tile_orbital, tile_window, tile_count, tile_values)
     tiles, parts = gather(payload, pieces)
     rows = [part[start + BODY:start + BODY + 1, :64] for part in tiles for start in range(0, part.shape[0], PAY)]

time: 104 us -> 104 us (level)
  local copies, waits for them, and re-layouts: 6.09 us -> 1.66 us
  starting transfers between devices: 31.7 us -> 35 us
  Pallas kernels: 17.8 us -> 19.4 us
  waiting for transfers between devices: 43.7 us -> 44.9 us
    ppermute x20 -> x23, starting transfers between devices: 31.7 us -> 35 us  [permute(): return lax.ppermute(value, AXES, pairs)]
    unnamed x13 -> x4, local copies, waits for them, and re-layouts: 4.46 us -> 1.5 us
    pallas_call x0 -> x1, Pallas kernels: none -> 1.7 us  [cut_pieces(): pl.pallas_call(cut_kernel, out_shape=jax.ShapeDtypeStruct((2 * PIECE, 2 *...]
    concatenate x3 -> x0, other arithmetic: 1.69 us -> none  [the longest x1 0.96 us: gather(): near = swap_core(jnp.concatenate([first, above, below], axis=0))]
    slice x2 -> x1, local copies, waits for them, and re-layouts: 1.32 us -> 0.01 us  [gather(): single = first[:PIECE]]
    ppermute x20 -> x23, waiting for transfers between devices: 43.7 us -> 44.9 us  [permute(): return lax.ppermute(value, AXES, pairs)]
  transfers between devices with their start and end apart: 20 -> 23, of which waited for: 15 -> 13; matrix products, arithmetic and copies ran while one was open for 4% -> 1% of each run, Pallas kernels for 0% -> 0%
where the time goes in v4:
time: 104 us
  waiting for transfers between devices  44.9 us (43%)
  starting transfers between devices  35 us (34%)
  Pallas kernels  19.4 us (19%)
  other arithmetic  2.33 us (2%)
  local copies, waits for them, and re-layouts  1.66 us (2%)
    ppermute x23, waiting for transfers between devices, permute(): return lax.ppermute(value, AXES, pairs)  44.9 us
    ppermute x23, starting transfers between devices, permute(): return lax.ppermute(value, AXES, pairs)  35 us
    pallas_call x1, Pallas kernels, chi_call(): pl.pallas_call(chi_kernel, out_shape=(jax.ShapeDtypeStruct((128, RW), F32...  15.6 us
  transfers between devices with their start and end apart: 23, of which 13 were waited for; matrix products, arithmetic and copies ran while one was open for 1% of the time, Pallas kernels for 0%

profile of v4, /device:TPU:6, one launch (start us, length us, event | category | flops | bytes accessed | tf_op | source)
XLA Modules:
  0.0 104.1 jit_solution(5860044903562594641)
XLA Ops:
  0.7 1.7 %shard_map.64 = bf16[512,256]{1,0:T(8,128)(2,1)} custom-call(bf16[2048,128]{1,0:T(8,128)(2,1)} %occ_ref.1, bf16[2048,128]{1,0:T(8,128)(2,1)} %vir_ref.1), custom_call_target="tpu_custom_call" | custom-call | tf_op jit(solution)/shard_map/pallas_call | solution.py:96
  2.4 2.1 %shard_map.65 = bf16[1040,128]{1,0:T(8,128)(2,1)} custom-call(s32[16]{0:T(128)} %orbital_ref.1, s32[16]{0:T(128)} %window_ref.1, s32[1]{0:T(128)S(6)} %copy.7.count_ref, bf16[16,64,128]{2,1,0:T(8,128)(2,1)} %tile_ref), custom_call_target="tpu_custom_call" | custom-call | tf_op jit(solution)/shard_map/pallas_call | solution.py:138
  4.4 0.8 collective-permute-start
  5.3 4.6 %collective-permute-start.1 = (bf16[512,256]{1,0:T(8,128)(2,1)}, bf16[512,256]{1,0:T(8,128)(2,1)S(1)}, u32[]{:S(2)}, u32[]{:S(2)}) collective-permute-start(bf16[512,256]{1,0:T(8,128)(2,1)} %shard_map.64), channel_id=1, source_target_pairs={{0,48},{1,96},{2,176},{3,224},{4,16},{5,80},{6,144},{7,208},{8,112... | collective-permute-start | bytes 786440 | tf_op jit(solution)/shard_map/ppermute | solution.py:38
  9.9 2.9 %collective-permute-done = bf16[1040,128]{1,0:T(8,128)(2,1)S(1)} collective-permute-done((bf16[1040,128]{1,0:T(8,128)(2,1)}, bf16[1040,128]{1,0:T(8,128)(2,1)S(1)}, u32[]{:S(2)}, u32[]{:S(2)}) %collective-permute-start) | collective-permute-done | bytes 266272 | tf_op jit(solution)/shard_map/ppermute | solution.py:38
  12.8 1.0 pad_maximum_fusion.refs_0_
  13.8 0.4 collective-permute-done.1.refs_5_
  14.1 9.8 %collective-permute-start.7 = (bf16[2080,128]{1,0:T(8,128)(2,1)S(1)}, bf16[2080,128]{1,0:T(8,128)(2,1)S(1)}, u32[]{:S(2)}, u32[]{:S(2)}) collective-permute-start(bf16[2080,128]{1,0:T(8,128)(2,1)S(1)} %pad_maximum_fusion.refs_0_), channel_id=1, source_target_pairs={{0,12},{1,13},{2,14},{3,15},{4,0},{5,1},{6,2},{7,3},{8,4},{9,5},{1... | collective-permute-start | bytes 1597448 | tf_op jit(solution)/shard_map/ppermute | solution.py:38
  23.9 0.0 collective-permute-start.6
  23.9 1.0 collective-permute-start.5
  24.9 0.0 collective-permute-start.3
  24.9 4.4 %collective-permute-start.2 = (bf16[512,256]{1,0:T(8,128)(2,1)S(1)}, bf16[512,256]{1,0:T(8,128)(2,1)S(1)}, u32[]{:S(2)}, u32[]{:S(2)}) collective-permute-start(bf16[512,256]{1,0:T(8,128)(2,1)S(1)} %collective-permute-done.1.refs_5_), channel_id=1, source_target_pairs={{0,112},{1,113},{2,114},{3,115},{4,116},{5,117},{6,118},{7,119},{8... | collective-permute-start | bytes 786440 | tf_op jit(solution)/shard_map/ppermute | solution.py:38
  29.3 2.1 %collective-permute-done.5.refs_9_ = bf16[256,256]{1,0:T(8,128)(2,1)} collective-permute-done((bf16[256,256]{1,0:T(8,128)(2,1)S(1)}, bf16[256,256]{1,0:T(8,128)(2,1)}, u32[]{:S(2)}, u32[]{:S(2)}) %collective-permute-start.5) | collective-permute-done | bytes 131104 | tf_op jit(solution)/shard_map/ppermute | solution.py:38
  31.5 2.8 %collective-permute-start.4 = (bf16[256,256]{1,0:T(8,128)(2,1)S(1)}, bf16[256,256]{1,0:T(8,128)(2,1)S(1)}, u32[]{:S(2)}, u32[]{:S(2)}) collective-permute-start(bf16[256,256]{1,0:T(8,128)(2,1)S(1)} %slice.96), channel_id=1, source_target_pairs={{0,96},{1,97},{2,98},{3,99},{4,100},{5,101},{6,102},{7,103},{8,104... | collective-permute-start | bytes 393224 | tf_op jit(solution)/shard_map/ppermute | solution.py:38
  34.3 8.0 %collective-permute-done.4.refs_8_ = bf16[256,256]{1,0:T(8,128)(2,1)S(1)} collective-permute-done((bf16[256,256]{1,0:T(8,128)(2,1)S(1)}, bf16[256,256]{1,0:T(8,128)(2,1)S(1)}, u32[]{:S(2)}, u32[]{:S(2)}) %collective-permute-start.4) | collective-permute-done | bytes 131104 | tf_op jit(solution)/shard_map/ppermute | solution.py:38
  42.3 0.0 copy-start
  42.3 0.0 collective-permute-done.3.refs_7_
  42.3 0.0 collective-permute-done.2.refs_6_
  42.3 0.0 collective-permute-done.7.refs_2_
  42.3 0.0 collective-permute-done.6.refs_1_
  42.3 0.6 copy-done
  42.9 2.2 %collective-permute-start.9 = (bf16[1040,128]{1,0:T(8,128)(2,1)S(1)}, bf16[1040,128]{1,0:T(8,128)(2,1)S(1)}, u32[]{:S(2)}, u32[]{:S(2)}) collective-permute-start(bf16[1040,128]{1,0:T(8,128)(2,1)S(1)} %slice.103), channel_id=1, source_target_pairs={{0,12},{1,13},{2,14},{3,15},{4,0},{5,1},{6,2},{7,3},{8,4},{9,5},{1... | collective-permute-start | bytes 798728 | tf_op jit(solution)/shard_map/ppermute | solution.py:38
  45.1 0.0 collective-permute-start.8
  45.1 0.1 pad_add_fusion.place_ref
  45.2 0.0 collective-permute-start.10
  45.2 0.5 collective-permute-start.11
  45.7 0.1 collective-permute-start.12
  45.8 5.1 %collective-permute-done.9.refs_4_ = bf16[1040,128]{1,0:T(8,128)(2,1)S(1)} collective-permute-done((bf16[1040,128]{1,0:T(8,128)(2,1)S(1)}, bf16[1040,128]{1,0:T(8,128)(2,1)S(1)}, u32[]{:S(2)}, u32[]{:S(2)}) %collective-permute-start.9) | collective-permute-done | bytes 266272 | tf_op jit(solution)/shard_map/ppermute | solution.py:38
  50.9 0.0 collective-permute-start.13
  50.9 3.4 %collective-permute-done.8.refs_3_ = bf16[1040,128]{1,0:T(8,128)(2,1)S(1)} collective-permute-done((bf16[1040,128]{1,0:T(8,128)(2,1)S(1)}, bf16[1040,128]{1,0:T(8,128)(2,1)S(1)}, u32[]{:S(2)}, u32[]{:S(2)}) %collective-permute-start.8) | collective-permute-done | bytes 266272 | tf_op jit(solution)/shard_map/ppermute | solution.py:38
  54.3 0.0 collective-permute-start.14
  54.4 0.0 collective-permute-done.13.refs_13_
  54.4 1.6 %collective-permute-done.14.refs_14_ = bf16[256,256]{1,0:T(8,128)(2,1)} collective-permute-done((bf16[256,256]{1,0:T(8,128)(2,1)}, bf16[256,256]{1,0:T(8,128)(2,1)}, u32[]{:S(2)}, u32[]{:S(2)}) %collective-permute-start.14) | collective-permute-done | bytes 131104 | tf_op jit(solution)/shard_map/ppermute | solution.py:38
  56.0 0.0 collective-permute-done.10.refs_10_
  56.0 0.0 collective-permute-done.11.refs_11_
  56.0 0.0 collective-permute-done.12.refs_12_
  56.0 0.0 copy-start.1
  56.0 0.9 copy-done.1
  56.9 15.6 %shard_map.66 = (f32[128,1024]{1,0:T(8,128)S(1)}, f32[128,1024]{1,0:T(8,128)S(1)}, f32[128,1024]{1,0:T(8,128)S(1)}, f32[128,1024]{1,0:T(8,128)S(1)}, bf16[512,1024]{1,0:T(8,128)(2,1)S(1)}) custom-call(s32[4]{0:T(128)S(1)} %pad_add_fusion.place_ref, s32[8,64]{1,0:T(8,128)S(1)} %convert_element_type.43.meta_ref, ...), custom_call_target="tpu_custom_call" | custom-call | flops 12000000000 | bytes 8388608 | tf_op jit(solution)/shard_map/pallas_call | solution.py:249
  72.5 0.1 collective-permute-start.15
  72.6 2.6 %collective-permute-done.15 = bf16[512,1024]{1,0:T(8,128)(2,1)S(1)} collective-permute-done((bf16[512,1024]{1,0:T(8,128)(2,1)S(1)}, bf16[512,1024]{1,0:T(8,128)(2,1)S(1)}, u32[]{:S(2)}, u32[]{:S(2)}) %collective-permute-start.15) | collective-permute-done | bytes 1048608 | tf_op jit(solution)/shard_map/ppermute | solution.py:38
  75.3 0.2 convert_add_fusion.2
  75.6 0.6 collective-permute-start.18
  76.1 1.6 %collective-permute-start.16 = (bf16[64,1024]{1,0:T(8,128)(2,1)S(1)}, bf16[64,1024]{1,0:T(8,128)(2,1)S(1)}, u32[]{:S(2)}, u32[]{:S(2)}) collective-permute-start(bf16[64,1024]{1,0:T(8,128)(2,1)S(1)} %get-tuple-element.51), channel_id=1, source_target_pairs={{0,4},{1,5},{2,6},{3,7},{4,8},{5,9},{6,10},{7,11},{8,12},{9,13},{1... | collective-permute-start | bytes 393224 | tf_op jit(solution)/shard_map/ppermute | solution.py:38
  77.8 3.4 %collective-permute-done.18 = bf16[64,1024]{1,0:T(8,128)(2,1)S(1)} collective-permute-done((bf16[64,1024]{1,0:T(8,128)(2,1)S(1)}, bf16[64,1024]{1,0:T(8,128)(2,1)S(1)}, u32[]{:S(2)}, u32[]{:S(2)}) %collective-permute-start.18) | collective-permute-done | bytes 131104 | tf_op jit(solution)/shard_map/ppermute | solution.py:38
  81.2 1.8 %collective-permute-start.19 = (bf16[128,1024]{1,0:T(8,128)(2,1)S(1)}, bf16[128,1024]{1,0:T(8,128)(2,1)S(1)}, u32[]{:S(2)}, u32[]{:S(2)}) collective-permute-start(bf16[128,1024]{1,0:T(8,128)(2,1)S(1)} %pad_maximum_fusion.2), channel_id=1, source_target_pairs={{0,12},{1,13},{2,14},{3,15},{4,0},{5,1},{6,2},{7,3},{8,4},{9,5},{1... | collective-permute-start | bytes 786440 | tf_op jit(solution)/shard_map/ppermute | solution.py:38
  83.0 0.0 collective-permute-done.16
  83.1 0.4 collective-permute-start.17
  83.5 5.3 %collective-permute-done.19 = bf16[128,1024]{1,0:T(8,128)(2,1)S(1)} collective-permute-done((bf16[128,1024]{1,0:T(8,128)(2,1)S(1)}, bf16[128,1024]{1,0:T(8,128)(2,1)S(1)}, u32[]{:S(2)}, u32[]{:S(2)}) %collective-permute-start.19) | collective-permute-done | bytes 262176 | tf_op jit(solution)/shard_map/ppermute | solution.py:38
  88.8 2.8 %collective-permute-done.17 = bf16[128,1024]{1,0:T(8,128)(2,1)S(1)} collective-permute-done((bf16[128,1024]{1,0:T(8,128)(2,1)S(1)}, bf16[128,1024]{1,0:T(8,128)(2,1)S(1)}, u32[]{:S(2)}, u32[]{:S(2)}) %collective-permute-start.17) | collective-permute-done | bytes 262176 | tf_op jit(solution)/shard_map/ppermute | solution.py:38
  91.6 0.2 fusion.2
  91.8 3.0 %collective-permute-start.22 = (bf16[32,1024]{1,0:T(8,128)(2,1)S(1)}, bf16[32,1024]{1,0:T(8,128)(2,1)S(1)}, u32[]{:S(2)}, u32[]{:S(2)}) collective-permute-start(bf16[32,1024]{1,0:T(8,128)(2,1)S(1)} %get-tuple-element.49), channel_id=1, source_target_pairs={{0,2},{1,3},{2,0},{3,1},{4,6},{5,7},{6,4},{7,5},{8,10},{9,11},{10,... | collective-permute-start | bytes 196616 | tf_op jit(solution)/shard_map/ppermute | solution.py:38
  94.8 0.0 collective-permute-start.20
  94.8 1.2 %collective-permute-start.21 = (bf16[32,1024]{1,0:T(8,128)(2,1)S(1)}, bf16[32,1024]{1,0:T(8,128)(2,1)S(1)}, u32[]{:S(2)}, u32[]{:S(2)}) collective-permute-start(bf16[32,1024]{1,0:T(8,128)(2,1)S(1)} %get-tuple-element.50), channel_id=1, source_target_pairs={{0,18},{1,19},{2,16},{3,17},{4,22},{5,23},{6,20},{7,21},{8,26},{9,... | collective-permute-start | bytes 196616 | tf_op jit(solution)/shard_map/ppermute | solution.py:38
  96.0 1.4 %collective-permute-done.22 = bf16[32,1024]{1,0:T(8,128)(2,1)S(1)} collective-permute-done((bf16[32,1024]{1,0:T(8,128)(2,1)S(1)}, bf16[32,1024]{1,0:T(8,128)(2,1)S(1)}, u32[]{:S(2)}, u32[]{:S(2)}) %collective-permute-start.22) | collective-permute-done | bytes 65568 | tf_op jit(solution)/shard_map/ppermute | solution.py:38
  97.5 5.9 %collective-permute-done.20 = bf16[32,1024]{1,0:T(8,128)(2,1)S(1)} collective-permute-done((bf16[32,1024]{1,0:T(8,128)(2,1)S(1)}, bf16[32,1024]{1,0:T(8,128)(2,1)S(1)}, u32[]{:S(2)}, u32[]{:S(2)}) %collective-permute-start.20) | collective-permute-done | bytes 65568 | tf_op jit(solution)/shard_map/ppermute | solution.py:38
  103.3 0.0 collective-permute-done.21
  103.4 0.7 pad_maximum_fusion.3
  (20 shorter events, 0.3 us)
Async XLA Ops:
  4.4 8.3 %collective-permute-start = (bf16[1040,128]{1,0:T(8,128)(2,1)}, bf16[1040,128]{1,0:T(8,128)(2,1)S(1)}, u32[]{:S(2)}, u32[]{:S(2)}) collective-permute-start(bf16[1040,128]{1,0:T(8,128)(2,1)} %shard_map.65), channel_id=1, source_target_pairs={{0,2},{1,3},{2,0},{3,1},{4,6},{5,7},{6,4},{7,5},{8,10},{9,11},{10,... | collective-permute-start | bytes 798728 | tf_op jit(solution)/shard_map/ppermute | solution.py:38
  5.3 8.9 %collective-permute-start.1 = (bf16[512,256]{1,0:T(8,128)(2,1)}, bf16[512,256]{1,0:T(8,128)(2,1)S(1)}, u32[]{:S(2)}, u32[]{:S(2)}) collective-permute-start(bf16[512,256]{1,0:T(8,128)(2,1)} %shard_map.64), channel_id=1, source_target_pairs={{0,48},{1,96},{2,176},{3,224},{4,16},{5,80},{6,144},{7,208},{8,112... | collective-permute-start | bytes 786440 | tf_op jit(solution)/shard_map/ppermute | solution.py:38
  14.1 28.1 %collective-permute-start.7 = (bf16[2080,128]{1,0:T(8,128)(2,1)S(1)}, bf16[2080,128]{1,0:T(8,128)(2,1)S(1)}, u32[]{:S(2)}, u32[]{:S(2)}) collective-permute-start(bf16[2080,128]{1,0:T(8,128)(2,1)S(1)} %pad_maximum_fusion.refs_0_), channel_id=1, source_target_pairs={{0,12},{1,13},{2,14},{3,15},{4,0},{5,1},{6,2},{7,3},{8,4},{9,5},{1... | collective-permute-start | bytes 1597448 | tf_op jit(solution)/shard_map/ppermute | solution.py:38
  23.9 18.4 %collective-permute-start.6 = (bf16[2080,128]{1,0:T(8,128)(2,1)S(1)}, bf16[2080,128]{1,0:T(8,128)(2,1)S(1)}, u32[]{:S(2)}, u32[]{:S(2)}) collective-permute-start(bf16[2080,128]{1,0:T(8,128)(2,1)S(1)} %pad_maximum_fusion.refs_0_), channel_id=1, source_target_pairs={{0,4},{1,5},{2,6},{3,7},{4,8},{5,9},{6,10},{7,11},{8,12},{9,13},{1... | collective-permute-start | bytes 1597448 | tf_op jit(solution)/shard_map/ppermute | solution.py:38
  23.9 7.5 %collective-permute-start.5 = (bf16[256,256]{1,0:T(8,128)(2,1)S(1)}, bf16[256,256]{1,0:T(8,128)(2,1)}, u32[]{:S(2)}, u32[]{:S(2)}) collective-permute-start(bf16[256,256]{1,0:T(8,128)(2,1)S(1)} %slice.96), channel_id=1, source_target_pairs={{0,32},{1,33},{2,34},{3,35},{4,36},{5,37},{6,38},{7,39},{8,40},{9,... | collective-permute-start | bytes 393224 | tf_op jit(solution)/shard_map/ppermute | solution.py:38
  24.9 17.3 %collective-permute-start.3 = (bf16[512,256]{1,0:T(8,128)(2,1)S(1)}, bf16[512,256]{1,0:T(8,128)(2,1)S(1)}, u32[]{:S(2)}, u32[]{:S(2)}) collective-permute-start(bf16[512,256]{1,0:T(8,128)(2,1)S(1)} %collective-permute-done.1.refs_5_), channel_id=1, source_target_pairs={{0,16},{1,17},{2,18},{3,19},{4,20},{5,21},{6,22},{7,23},{8,24},{9,... | collective-permute-start | bytes 786440 | tf_op jit(solution)/shard_map/ppermute | solution.py:38
  24.9 17.3 %collective-permute-start.2 = (bf16[512,256]{1,0:T(8,128)(2,1)S(1)}, bf16[512,256]{1,0:T(8,128)(2,1)S(1)}, u32[]{:S(2)}, u32[]{:S(2)}) collective-permute-start(bf16[512,256]{1,0:T(8,128)(2,1)S(1)} %collective-permute-done.1.refs_5_), channel_id=1, source_target_pairs={{0,112},{1,113},{2,114},{3,115},{4,116},{5,117},{6,118},{7,119},{8... | collective-permute-start | bytes 786440 | tf_op jit(solution)/shard_map/ppermute | solution.py:38
  31.5 10.8 %collective-permute-start.4 = (bf16[256,256]{1,0:T(8,128)(2,1)S(1)}, bf16[256,256]{1,0:T(8,128)(2,1)S(1)}, u32[]{:S(2)}, u32[]{:S(2)}) collective-permute-start(bf16[256,256]{1,0:T(8,128)(2,1)S(1)} %slice.96), channel_id=1, source_target_pairs={{0,96},{1,97},{2,98},{3,99},{4,100},{5,101},{6,102},{7,103},{8,104... | collective-permute-start | bytes 393224 | tf_op jit(solution)/shard_map/ppermute | solution.py:38
  42.3 0.7 copy-start
  42.9 7.9 %collective-permute-start.9 = (bf16[1040,128]{1,0:T(8,128)(2,1)S(1)}, bf16[1040,128]{1,0:T(8,128)(2,1)S(1)}, u32[]{:S(2)}, u32[]{:S(2)}) collective-permute-start(bf16[1040,128]{1,0:T(8,128)(2,1)S(1)} %slice.103), channel_id=1, source_target_pairs={{0,12},{1,13},{2,14},{3,15},{4,0},{5,1},{6,2},{7,3},{8,4},{9,5},{1... | collective-permute-start | bytes 798728 | tf_op jit(solution)/shard_map/ppermute | solution.py:38
  45.1 9.2 %collective-permute-start.8 = (bf16[1040,128]{1,0:T(8,128)(2,1)S(1)}, bf16[1040,128]{1,0:T(8,128)(2,1)S(1)}, u32[]{:S(2)}, u32[]{:S(2)}) collective-permute-start(bf16[1040,128]{1,0:T(8,128)(2,1)S(1)} %slice.101), channel_id=1, source_target_pairs={{0,4},{1,5},{2,6},{3,7},{4,8},{5,9},{6,10},{7,11},{8,12},{9,13},{1... | collective-permute-start | bytes 798728 | tf_op jit(solution)/shard_map/ppermute | solution.py:38
  45.2 10.8 %collective-permute-start.10 = (bf16[512,256]{1,0:T(8,128)(2,1)S(1)}, bf16[512,256]{1,0:T(8,128)(2,1)S(1)}, u32[]{:S(2)}, u32[]{:S(2)}) collective-permute-start(bf16[512,256]{1,0:T(8,128)(2,1)S(1)} %collective-permute-done.1.refs_5_), channel_id=1, source_target_pairs={{0,1},{1,0},{2,3},{3,2},{4,5},{5,4},{6,7},{7,6},{8,9},{9,8},{10,11... | collective-permute-start | bytes 786440 | tf_op jit(solution)/shard_map/ppermute | solution.py:38
  45.2 10.8 %collective-permute-start.11 = (bf16[512,256]{1,0:T(8,128)(2,1)S(1)}, bf16[512,256]{1,0:T(8,128)(2,1)S(1)}, u32[]{:S(2)}, u32[]{:S(2)}) collective-permute-start(bf16[512,256]{1,0:T(8,128)(2,1)S(1)} %collective-permute-done.2.refs_6_), channel_id=1, source_target_pairs={{0,1},{1,0},{2,3},{3,2},{4,5},{5,4},{6,7},{7,6},{8,9},{9,8},{10,11... | collective-permute-start | bytes 786440 | tf_op jit(solution)/shard_map/ppermute | solution.py:38
  45.7 10.3 %collective-permute-start.12 = (bf16[512,256]{1,0:T(8,128)(2,1)S(1)}, bf16[512,256]{1,0:T(8,128)(2,1)}, u32[]{:S(2)}, u32[]{:S(2)}) collective-permute-start(bf16[512,256]{1,0:T(8,128)(2,1)S(1)} %collective-permute-done.3.refs_7_), channel_id=1, source_target_pairs={{0,1},{1,0},{2,3},{3,2},{4,5},{5,4},{6,7},{7,6},{8,9},{9,8},{10,11... | collective-permute-start | bytes 786440 | tf_op jit(solution)/shard_map/ppermute | solution.py:38
  50.9 3.5 %collective-permute-start.13 = (bf16[256,256]{1,0:T(8,128)(2,1)}, bf16[256,256]{1,0:T(8,128)(2,1)}, u32[]{:S(2)}, u32[]{:S(2)}) collective-permute-start(bf16[256,256]{1,0:T(8,128)(2,1)} %copy-done), channel_id=1, source_target_pairs={{0,1},{1,0},{2,3},{3,2},{4,5},{5,4},{6,7},{7,6},{8,9},{9,8},{10,11... | collective-permute-start | bytes 393224 | tf_op jit(solution)/shard_map/ppermute | solution.py:38
  54.3 1.7 %collective-permute-start.14 = (bf16[256,256]{1,0:T(8,128)(2,1)}, bf16[256,256]{1,0:T(8,128)(2,1)}, u32[]{:S(2)}, u32[]{:S(2)}) collective-permute-start(bf16[256,256]{1,0:T(8,128)(2,1)} %collective-permute-done.5.refs_9_), channel_id=1, source_target_pairs={{0,1},{1,0},{2,3},{3,2},{4,5},{5,4},{6,7},{7,6},{8,9},{9,8},{10,11... | collective-permute-start | bytes 393224 | tf_op jit(solution)/shard_map/ppermute | solution.py:38
  56.0 0.9 copy-start.1
  72.5 2.7 %collective-permute-start.15 = (bf16[512,1024]{1,0:T(8,128)(2,1)S(1)}, bf16[512,1024]{1,0:T(8,128)(2,1)S(1)}, u32[]{:S(2)}, u32[]{:S(2)}) collective-permute-start(bf16[512,1024]{1,0:T(8,128)(2,1)S(1)} %get-tuple-element.33), channel_id=1, source_target_pairs={{0,1},{1,0},{2,3},{3,2},{4,5},{5,4},{6,7},{7,6},{8,9},{9,8},{10,11... | collective-permute-start | bytes 3145736 | tf_op jit(solution)/shard_map/ppermute | solution.py:38
  75.6 5.6 %collective-permute-start.18 = (bf16[64,1024]{1,0:T(8,128)(2,1)S(1)}, bf16[64,1024]{1,0:T(8,128)(2,1)S(1)}, u32[]{:S(2)}, u32[]{:S(2)}) collective-permute-start(bf16[64,1024]{1,0:T(8,128)(2,1)S(1)} %get-tuple-element.52), channel_id=1, source_target_pairs={{0,12},{1,13},{2,14},{3,15},{4,0},{5,1},{6,2},{7,3},{8,4},{9,5},{1... | collective-permute-start | bytes 393224 | tf_op jit(solution)/shard_map/ppermute | solution.py:38
  76.1 6.9 %collective-permute-start.16 = (bf16[64,1024]{1,0:T(8,128)(2,1)S(1)}, bf16[64,1024]{1,0:T(8,128)(2,1)S(1)}, u32[]{:S(2)}, u32[]{:S(2)}) collective-permute-start(bf16[64,1024]{1,0:T(8,128)(2,1)S(1)} %get-tuple-element.51), channel_id=1, source_target_pairs={{0,4},{1,5},{2,6},{3,7},{4,8},{5,9},{6,10},{7,11},{8,12},{9,13},{1... | collective-permute-start | bytes 393224 | tf_op jit(solution)/shard_map/ppermute | solution.py:38
  81.2 7.6 %collective-permute-start.19 = (bf16[128,1024]{1,0:T(8,128)(2,1)S(1)}, bf16[128,1024]{1,0:T(8,128)(2,1)S(1)}, u32[]{:S(2)}, u32[]{:S(2)}) collective-permute-start(bf16[128,1024]{1,0:T(8,128)(2,1)S(1)} %pad_maximum_fusion.2), channel_id=1, source_target_pairs={{0,12},{1,13},{2,14},{3,15},{4,0},{5,1},{6,2},{7,3},{8,4},{9,5},{1... | collective-permute-start | bytes 786440 | tf_op jit(solution)/shard_map/ppermute | solution.py:38
  83.1 8.5 %collective-permute-start.17 = (bf16[128,1024]{1,0:T(8,128)(2,1)S(1)}, bf16[128,1024]{1,0:T(8,128)(2,1)S(1)}, u32[]{:S(2)}, u32[]{:S(2)}) collective-permute-start(bf16[128,1024]{1,0:T(8,128)(2,1)S(1)} %pad_maximum_fusion.1), channel_id=1, source_target_pairs={{0,4},{1,5},{2,6},{3,7},{4,8},{5,9},{6,10},{7,11},{8,12},{9,13},{1... | collective-permute-start | bytes 786440 | tf_op jit(solution)/shard_map/ppermute | solution.py:38
  91.8 5.7 %collective-permute-start.22 = (bf16[32,1024]{1,0:T(8,128)(2,1)S(1)}, bf16[32,1024]{1,0:T(8,128)(2,1)S(1)}, u32[]{:S(2)}, u32[]{:S(2)}) collective-permute-start(bf16[32,1024]{1,0:T(8,128)(2,1)S(1)} %get-tuple-element.49), channel_id=1, source_target_pairs={{0,2},{1,3},{2,0},{3,1},{4,6},{5,7},{6,4},{7,5},{8,10},{9,11},{10,... | collective-permute-start | bytes 196616 | tf_op jit(solution)/shard_map/ppermute | solution.py:38
  94.8 8.5 %collective-permute-start.20 = (bf16[32,1024]{1,0:T(8,128)(2,1)S(1)}, bf16[32,1024]{1,0:T(8,128)(2,1)S(1)}, u32[]{:S(2)}, u32[]{:S(2)}) collective-permute-start(bf16[32,1024]{1,0:T(8,128)(2,1)S(1)} %get-tuple-element.48), channel_id=1, source_target_pairs={{0,16},{1,17},{2,18},{3,19},{4,20},{5,21},{6,22},{7,23},{8,24},{9,... | collective-permute-start | bytes 196616 | tf_op jit(solution)/shard_map/ppermute | solution.py:38
  94.8 8.5 %collective-permute-start.21 = (bf16[32,1024]{1,0:T(8,128)(2,1)S(1)}, bf16[32,1024]{1,0:T(8,128)(2,1)S(1)}, u32[]{:S(2)}, u32[]{:S(2)}) collective-permute-start(bf16[32,1024]{1,0:T(8,128)(2,1)S(1)} %get-tuple-element.50), channel_id=1, source_target_pairs={{0,18},{1,19},{2,16},{3,17},{4,22},{5,23},{6,20},{7,21},{8,26},{9,... | collective-permute-start | bytes 196616 | tf_op jit(solution)/shard_map/ppermute | solution.py:38
